TPU v7x, 32 devices: a whole 2x2x4 slice. The times are simulated.
32 devices in a mesh: dp: 8 (over z, core), heads: 2 (over x), expert: 2 (over y).
Axes of the slice: x: 2, y: 2, z: 4, core: 2. Of those that a mesh axis runs over, the one named last changes fastest.
Arguments:
- block_in: bfloat16 [64, 197, 768], P(('dp', 'expert'), None, 'heads'), may hold values from -6 to 6
- cotangent: bfloat16 [64, 197, 768], P(('dp', 'expert'), None, 'heads'), may hold values from -8 to 8
- route_ids: int32 [64, 197, 2], P(('dp', 'expert')), may hold values from 0 to 7, all different within a row; in each aligned block of 788 rows (0 to 787, 788 to 1575, ..., all dimensions but the last counted through in order) at most 281 rows name the same one
- gain_attn: bfloat16 [768], P(('dp', 'expert')), may hold values from 0.099609375 to 1.8984375
- w_qkv: bfloat16 [768, 3, 768], P(('dp', 'expert'), None, 'heads'), may hold values from -0.21875 to 0.21875
- w_out_attn: bfloat16 [768, 768], P(('dp', 'expert'), 'heads'), may hold values from -0.875 to 0.875
- gain_moe: bfloat16 [768], P(('dp', 'expert')), may hold values from 0.099609375 to 1.8984375
- router: bfloat16 [768, 8], P(('dp', 'expert')), may hold values from -0.21875 to 0.21875
- w_in: bfloat16 [768, 8, 3072], P('dp', 'expert', 'heads'), may hold values from -0.21875 to 0.21875
- w_out: bfloat16 [768, 8, 3072], P('dp', 'expert', 'heads'), may hold values from -2.5 to 2.5
Outputs:
- block_out: bfloat16 [64, 197, 768], P(('dp', 'expert'), None, 'heads')
- grad_block_in: bfloat16 [64, 197, 768], P(('dp', 'expert'), None, 'heads')
- grad_gain_attn: float32 [768], P(('dp', 'expert'))
- grad_w_qkv: float32 [768, 3, 768], P(('dp', 'expert'), None, 'heads')
- grad_w_out_attn: float32 [768, 768], P(('dp', 'expert'), 'heads')
- grad_gain_moe: float32 [768], P(('dp', 'expert'))
- grad_router: float32 [768, 8], P(('dp', 'expert'))
- grad_w_in: float32 [768, 8, 3072], P('dp', 'expert', 'heads')
- grad_w_out: float32 [768, 8, 3072], P('dp', 'expert', 'heads')
Inputs may be any that keep to these rules, and one draw needn't show every extreme that they name: `route_ids`: each token names two different experts. Within each aligned block of 788 tokens (the images of one index of dp and expert) no expert is named more than 281 times, a bound that some block reaches.
All inputs are finite; a program needn't handle non-finite values.
Results may differ from a plain program's by a relative error of at most 0.022.
Values may be sent and summed in bfloat16 or wider, within the bound.
No kernel may reach another device: no remote copies, remote signals or barrier semaphores. Data moves between devices by JAX's collectives and lax.ppermute only.
A program may use at most 192 MiB of HBM per device.

v0:
```python
import functools

import jax
import jax.numpy as jnp
from jax import lax
from jax.experimental import pallas as pl
from jax.experimental.pallas import tpu as pltpu
from jax.sharding import PartitionSpec as P

HEAD_DIM = 64
CORES = 2
EPS = 1e-06
LOW = -1e30
F32 = jnp.float32
BF16 = jnp.bfloat16
VMEM_LIMIT = 56 * 1024 * 1024
SHARE = 64


def dot(a, b, ca, cb):
    return lax.dot_general(a, b, (((ca,), (cb,)), ((), ())), preferred_element_type=F32)


def shaped(shape, kind):
    return jax.ShapeDtypeStruct(shape, kind)


def params(dims=1):
    return pltpu.CompilerParams(
        dimension_semantics=("arbitrary",) * dims, vmem_limit_bytes=VMEM_LIMIT
    )


def cost(flops, size, powers=0):
    return pl.CostEstimate(
        flops=flops // SHARE, bytes_accessed=size // SHARE, transcendentals=powers // SHARE
    )


def after(value, *others):
    return lax.optimization_barrier((value,) + others)[0]


def norm_parts(rows):
    average = jnp.mean(rows, axis=-1, keepdims=True)
    centred = rows - average
    spread = jnp.mean(centred * centred, axis=-1, keepdims=True)
    scale = lax.rsqrt(spread + EPS)
    return centred * scale, scale


def softmax_rows(q, own_k, real):
    scores = jnp.where(real, dot(q, own_k, 1, 1) * (HEAD_DIM**-0.5), LOW)
    powers = jnp.exp(scores - jnp.max(scores, axis=-1, keepdims=True))
    return powers / jnp.sum(powers, axis=-1, keepdims=True)


def attend_kernel(seq, x_ref, gain_ref, wqkv_ref, wo_ref, part_ref, qkv_ref, ctx_ref):
    width = wo_ref.shape[1]
    span = x_ref.shape[0]
    unit, _ = norm_parts(x_ref[...].astype(F32))
    normed = (unit * gain_ref[...]).astype(BF16)
    for part in range(3):
        cols = slice(part * width, (part + 1) * width)
        qkv_ref[:, cols] = dot(normed, wqkv_ref[:, cols], 1, 0).astype(BF16)
    lane = lax.broadcasted_iota(jnp.int32, (span, 128), 1)
    real = lax.broadcasted_iota(jnp.int32, (span, span), 1) < seq
    for pair in range(width // 128):
        q, k, v = (
            qkv_ref[:, part * width + pair * 128 : part * width + (pair + 1) * 128]
            for part in range(3)
        )
        ctx = jnp.zeros((span, 128), F32)
        for side in range(2):
            mine = (lane >= 64) if side else (lane < 64)
            own_k = jnp.where(mine, k, jnp.zeros_like(k))
            own_v = jnp.where(mine, v, jnp.zeros_like(v))
            weights = softmax_rows(q, own_k, real)
            ctx = ctx + dot(weights.astype(BF16), own_v, 1, 0)
        ctx_ref[:, pair * 128 : (pair + 1) * 128] = ctx.astype(BF16)
    part_ref[...] = dot(ctx_ref[...], wo_ref[...], 1, 1).astype(BF16)


def attend(inputs, gain, packed, width, images, seq):
    rows, model = inputs.shape
    span = rows // images
    image = lambda last: pl.BlockSpec((span, last), lambda i: (i, 0))
    return pl.pallas_call(
        functools.partial(attend_kernel, seq),
        grid=(images,),
        in_specs=[
            image(model),
            pl.BlockSpec((1, model), lambda i: (0, 0)),
            pl.BlockSpec((model, 3 * width), lambda i: (0, 0)),
            pl.BlockSpec((model, width), lambda i: (0, 3)),
        ],
        out_specs=[image(model), image(3 * width), image(width)],
        out_shape=[
            shaped((rows, model), BF16), shaped((rows, 3 * width), BF16), shaped((rows, width), BF16)
        ],
        compiler_params=params(),
        cost_estimate=cost(10 * rows * model * width, 8 * rows * model, rows * span * width // 64),
        name="attend",
    )(inputs, gain, packed, packed)


def attend_back_kernel(
    seq, gain_at,
    x_ref, gain_ref, datt_ref, qkv_ref, ctx_ref, wqkv_ref, wo_ref, side_ref,
    dnorm_ref, stats_ref, pack_ref, dproj_ref, dgain_ref, dwqkv_ref, dwo_ref,
):
    width = wo_ref.shape[1]
    span, model = x_ref.shape
    step = pl.program_id(0)

    @pl.when(step == 0)
    def _():
        dgain_ref[...] = jnp.zeros_like(dgain_ref)
        dwqkv_ref[...] = jnp.zeros_like(dwqkv_ref)
        dwo_ref[...] = jnp.zeros_like(dwo_ref)

    datt = datt_ref[...]
    dwo_ref[...] += dot(datt, ctx_ref[...], 0, 0)
    dctx_all = dot(datt, wo_ref[...], 1, 0).astype(BF16)
    lane = lax.broadcasted_iota(jnp.int32, (span, 128), 1)
    real = lax.broadcasted_iota(jnp.int32, (span, span), 1) < seq
    for pair in range(width // 128):
        q, k, v = (
            qkv_ref[:, part * width + pair * 128 : part * width + (pair + 1) * 128]
            for part in range(3)
        )
        dctx = dctx_all[:, pair * 128 : (pair + 1) * 128]
        dq = jnp.zeros((span, 128), F32)
        dk = jnp.zeros((span, 128), F32)
        dv = jnp.zeros((span, 128), F32)
        for side in range(2):
            mine = (lane >= 64) if side else (lane < 64)
            own = lambda t: jnp.where(mine, t, jnp.zeros_like(t))
            own_k, own_v = own(k), own(v)
            weights = softmax_rows(q, own_k, real)
            dweights = dot(dctx, own_v, 1, 1)
            inner = jnp.sum(dweights * weights, axis=-1, keepdims=True)
            dscores = (weights * (dweights - inner)).astype(BF16)
            dq = dq + dot(dscores, own_k, 1, 0)
            dk = dk + dot(dscores, own(q), 0, 0)
            dv = dv + dot(weights.astype(BF16), own(dctx), 0, 0)
        for part, value in enumerate((dq * HEAD_DIM**-0.5, dk * HEAD_DIM**-0.5, dv)):
            start = part * width + pair * 128
            dproj_ref[:, start : start + 128] = value.astype(BF16)
    dproj = dproj_ref[...]
    gain = gain_ref[...]
    unit, _ = norm_parts(x_ref[...].astype(F32))
    normed = (unit * gain).astype(BF16)
    dwqkv_ref[...] += dot(normed, dproj, 0, 0)
    dnormed = dot(dproj, wqkv_ref[...], 1, 1)
    halves, _, half = dnorm_ref.shape
    for h in range(halves):
        dnorm_ref[h] = dnormed[:, h * half : (h + 1) * half].astype(BF16)
    along = dnormed * unit
    dgain_ref[...] += jnp.sum(along, axis=0, keepdims=True)
    first = jnp.sum(dnormed * gain, axis=-1, keepdims=True)
    second = jnp.sum(along * gain, axis=-1, keepdims=True)
    stats_ref[...] = jnp.where(lane == 0, first, jnp.where(lane == 1, second, 0.0))

    @pl.when(step == pl.num_programs(0) - 1)
    def _():
        pack_ref[:, : 3 * width] = dwqkv_ref[...].astype(BF16)
        pack_ref[:, 3 * width : 4 * width] = dwo_ref[...].astype(BF16)
        line = lax.broadcasted_iota(jnp.int32, (128, model), 0)
        column = jnp.where(line == gain_at, dgain_ref[...], 0.0).T
        pack_ref[:, 4 * width :] = (side_ref[...] + column).astype(BF16)


def attend_back(inputs, gain, datt, qkv, ctx, packed, dside, gain_at, width, images, seq, halves):
    rows, model = inputs.shape
    span = rows // images
    image = lambda last: pl.BlockSpec((span, last), lambda i: (i, 0))
    fixed = lambda *size: pl.BlockSpec(size, lambda i: (0, 0))
    return pl.pallas_call(
        functools.partial(attend_back_kernel, seq, gain_at),
        grid=(images,),
        in_specs=[
            image(model), fixed(1, model), image(model), image(3 * width), image(width),
            fixed(model, 3 * width), pl.BlockSpec((model, width), lambda i: (0, 3)),
            fixed(model, 128),
        ],
        out_specs=[
            pl.BlockSpec((halves, span, model // halves), lambda i: (0, i, 0)),
            image(128),
            fixed(*packed.shape),
        ],
        out_shape=[
            shaped((halves, rows, model // halves), BF16),
            shaped((rows, 128), F32),
            shaped(packed.shape, BF16),
        ],
        scratch_shapes=[
            pltpu.VMEM((span, 3 * width), BF16),
            pltpu.VMEM((1, model), F32),
            pltpu.VMEM((model, 3 * width), F32),
            pltpu.VMEM((model, width), F32),
        ],
        compiler_params=params(),
        cost_estimate=cost(28 * rows * model * width, 12 * rows * model, rows * span * width // 64),
        name="attend_back",
    )(inputs, gain, datt, qkv, ctx, packed, packed, dside)


def expert_kernel(depth, blocks, place_ref, slot_ref, router_ref, *refs):
    x_refs, refs = refs[:blocks], refs[blocks:]
    grad_refs, refs = refs[:blocks], refs[blocks:]
    win_refs, refs = refs[:depth], refs[depth:]
    wout_refs, refs = refs[:depth], refs[depth:]
    (
        rows_ref, mids_ref, dchosen_ref, drows_ref, yrows_ref, probs_ref, win_all, wout_all,
    ) = refs
    slots, model = rows_ref.shape[2:]
    tokens = x_refs[0].shape[0]
    part_rows, width = win_refs[0].shape[1:]
    step = pl.program_id(0)

    @pl.when(step == 0)
    def _():
        for k in range(depth):
            owner = lax.rem(place_ref[0] - k + depth, depth)
            at = pl.ds(pl.multiple_of(owner * part_rows, 16), part_rows)
            win_all[at, :] = win_refs[k][0]
            wout_all[at, :] = wout_refs[k][0]

    mask = lax.broadcasted_iota(jnp.int32, (slots, tokens), 0) == slot_ref[0]
    pick = jnp.where(mask, 1.0, 0.0).astype(BF16)
    for b in range(blocks):

        @pl.when(step == b)
        def _(b=b):
            rows_ref[0, 0] = dot(pick, grad_refs[b][...], 1, 0).astype(BF16)
            rows_ref[1, 0] = dot(pick, x_refs[b][...], 1, 0).astype(BF16)
            logits = dot(router_ref[...], x_refs[b][...], 1, 1)
            powers = jnp.exp(logits - jnp.max(logits, axis=0, keepdims=True))
            probs_ref[0] = powers / jnp.sum(powers, axis=0, keepdims=True)

    probs = probs_ref[0]
    line = lax.broadcasted_iota(jnp.int32, probs.shape, 0)
    own = jnp.sum(jnp.where(line == place_ref[1], probs, 0.0), axis=0, keepdims=True)
    gate = jnp.sum(jnp.where(mask, own, 0.0), axis=1, keepdims=True)
    grows, rows = rows_ref[0, 0], rows_ref[1, 0]
    dgate = jnp.zeros((slots, 1), F32)
    drows = jnp.zeros((slots, model), F32)
    yrows = jnp.zeros((slots, model), F32)
    tile = 512 if width % 512 == 0 else width
    curve = 0.7978845608028654
    for start in range(0, width, tile):
        cols = slice(start, start + tile)
        win, wout = win_all[:, cols], wout_all[:, cols]
        hidden = dot(rows, win, 1, 0)
        pulled = dot(grows, wout, 1, 0)
        square = hidden * hidden
        bend = jnp.tanh(hidden * (curve + curve * 0.044715 * square))
        half = 0.5 + 0.5 * bend
        active = hidden * half
        slope = half + 0.5 * hidden * (1.0 - bend * bend) * (
            curve + 3.0 * curve * 0.044715 * square
        )
        dgate = dgate + jnp.sum(active * pulled, axis=1, keepdims=True)
        gact = (gate * active).astype(BF16)
        dhid = (gate * pulled * slope).astype(BF16)
        mids_ref[0, 0, :, cols] = gact
        mids_ref[1, 0, :, cols] = dhid
        drows = drows + dot(dhid, win, 1, 1)
        yrows = yrows + dot(gact, wout, 1, 1)
    dchosen_ref[0] = jnp.sum(jnp.where(mask, dgate, 0.0), axis=0, keepdims=True)
    drows_ref[0] = drows.astype(BF16)
    yrows_ref[0] = yrows.astype(BF16)


def run_expert(place, slot_of, router_rows, xs, grads, pieces, slots):
    blocks, depth = len(xs), len(pieces)
    tokens, model = xs[0].shape
    _, part_rows, width = pieces[0].shape
    experts = router_rows.shape[0]
    fixed = lambda *size: pl.BlockSpec(
        size, lambda b, s: (0,) * len(size), pipeline_mode=pl.Buffered(1)
    )
    block = lambda *size: pl.BlockSpec((1,) + size, lambda b, s: (b, 0, 0))
    both = lambda last: pl.BlockSpec((2, 1, slots, last), lambda b, s: (0, b, 0, 0))
    weight = lambda which: pl.BlockSpec(
        (1, part_rows, width), lambda b, s: (which, 0, 0), pipeline_mode=pl.Buffered(1)
    )
    return pl.pallas_call(
        functools.partial(expert_kernel, depth, blocks),
        grid_spec=pltpu.PrefetchScalarGridSpec(
            num_scalar_prefetch=1,
            grid=(blocks,),
            in_specs=[block(1, tokens), fixed(experts, model)]
            + [fixed(tokens, model)] * (2 * blocks)
            + [weight(1)] * depth
            + [weight(0)] * depth,
            out_specs=[
                both(model), both(width), block(1, tokens), block(slots, model),
                block(slots, model), block(experts, tokens),
            ],
            scratch_shapes=[pltpu.VMEM((model, width), BF16)] * 2,
        ),
        out_shape=[
            shaped((2, blocks, slots, model), BF16), shaped((2, blocks, slots, width), BF16),
            shaped((blocks, 1, tokens), F32), shaped((blocks, slots, model), BF16),
            shaped((blocks, slots, model), BF16), shaped((blocks, experts, tokens), F32),
        ],
        compiler_params=params(),
        cost_estimate=cost(
            8 * blocks * slots * model * width + 4 * blocks * slots * model * tokens,
            16 * blocks * slots * model,
            blocks * slots * width,
        ),
        name="expert",
    )(place, slot_of, router_rows, *xs, *grads, *pieces, *pieces)


def weight_grad_kernel(depth, place_ref, rows_ref, cols_ref, *refs):
    out_refs, total_ref = refs[:depth], refs[depth]
    _, blocks, slots, model = rows_ref.shape
    width = cols_ref.shape[3]
    part_rows = model // depth
    left = rows_ref[0].reshape(blocks * slots, model)
    right = cols_ref[0].reshape(blocks * slots, width)
    total_ref[...] = dot(left, right, 0, 0)
    for k in range(depth):
        owner = lax.rem(place_ref[0] - k + depth, depth)
        at = pl.ds(pl.multiple_of(owner * part_rows, 16), part_rows)
        out_refs[k][0] = total_ref[at, :].astype(BF16)


def weight_grad(place, rows, cols, depth):
    _, blocks, slots, model = rows.shape
    width = cols.shape[3]
    both = lambda last: pl.BlockSpec((1, blocks, slots, last), lambda i, s: (i, 0, 0, 0))
    return pl.pallas_call(
        functools.partial(weight_grad_kernel, depth),
        grid_spec=pltpu.PrefetchScalarGridSpec(
            num_scalar_prefetch=1,
            grid=(2,),
            in_specs=[both(model), both(width)],
            out_specs=[pl.BlockSpec((1, model // depth, width), lambda i, s: (i, 0, 0))] * depth,
            scratch_shapes=[pltpu.VMEM((model, width), F32)],
        ),
        out_shape=[shaped((2, model // depth, width), BF16)] * depth,
        compiler_params=params(),
        cost_estimate=cost(
            4 * blocks * slots * model * width,
            4 * (blocks * slots * (model + width) + model * width),
        ),
        name="weight_grad",
    )(place, rows, cols)


def combine_kernel(local, added, slot_ref, *refs):
    rows_refs, refs = refs[:local], refs[local:]
    out_ref = refs[-1]
    tokens = out_ref.shape[-2]
    slots, model = rows_refs[0].shape[1:]
    at = lax.broadcasted_iota(jnp.int32, (tokens, slots), 1)
    total = refs[0][...].astype(F32) if added else jnp.zeros((tokens, model), F32)
    for e in range(local):
        pick = jnp.where(at == slot_ref[0, :, e : e + 1], 1.0, 0.0).astype(BF16)
        total = total + dot(pick, rows_refs[e][0], 1, 0)
    out_ref[...] = total.astype(BF16)


def combine(slot_cols, rows, b, add=None):
    _, tokens, local = slot_cols.shape
    slots, model = rows[0].shape[1:]
    whole = pl.BlockSpec((tokens, model), lambda i: (0, 0))
    return pl.pallas_call(
        functools.partial(combine_kernel, local, add is not None),
        grid=(1,),
        in_specs=[pl.BlockSpec((1, tokens, local), lambda i: (b, 0, 0))]
        + [pl.BlockSpec((1, slots, model), lambda i: (b, 0, 0))] * local
        + [whole] * (add is not None),
        out_specs=whole,
        out_shape=shaped((tokens, model), BF16),
        compiler_params=params(),
        cost_estimate=cost(
            2 * local * slots * model * tokens, 2 * model * (local * slots + 2 * tokens)
        ),
        name="combine",
    )(slot_cols, *rows, *(() if add is None else (add,)))


def combine_back_kernel(local, added, place_ref, slot_ref, *refs):
    rows_refs, refs = refs[:local], refs[local:]
    dchosen_refs, refs = refs[:local], refs[local:]
    probs_ref, router_ref, x_ref = refs[:3]
    out_ref, drouter_ref = refs[-2:]
    tokens = out_ref.shape[0]
    slots = rows_refs[0].shape[1]
    at = lax.broadcasted_iota(jnp.int32, (tokens, slots), 1)
    probs = probs_ref[0]
    line = lax.broadcasted_iota(jnp.int32, probs.shape, 0)
    dprobs = jnp.zeros_like(probs)
    for e in range(local):
        dprobs = jnp.where(line == place_ref[1] + e, dchosen_refs[e][0], dprobs)
    inner = jnp.sum(dprobs * probs, axis=0, keepdims=True)
    dlogits = (probs * (dprobs - inner)).astype(BF16)
    drouter_ref[...] = dot(dlogits, x_ref[...], 1, 0)
    total = dot(dlogits, router_ref[...], 0, 0)
    if added:
        total = total + refs[3][...].astype(F32)
    for e in range(local):
        pick = jnp.where(at == slot_ref[0, :, e : e + 1], 1.0, 0.0).astype(BF16)
        total = total + dot(pick, rows_refs[e][0], 1, 0)
    out_ref[...] = total.astype(BF16)


def combine_back(place, slot_cols, rows, dchosen, probs, router_rows, x, b, add=None):
    _, tokens, local = slot_cols.shape
    slots, model = rows[0].shape[1:]
    experts = router_rows.shape[0]
    whole = pl.BlockSpec((tokens, model), lambda i, s: (0, 0))
    block = lambda *size: pl.BlockSpec((1,) + size, lambda i, s: (b, 0, 0))
    small = pl.BlockSpec((experts, model), lambda i, s: (0, 0))
    return pl.pallas_call(
        functools.partial(combine_back_kernel, local, add is not None),
        grid_spec=pltpu.PrefetchScalarGridSpec(
            num_scalar_prefetch=1,
            grid=(1,),
            in_specs=[block(tokens, local)]
            + [block(slots, model)] * local
            + [block(1, tokens)] * local
            + [block(experts, tokens), small, whole]
            + [whole] * (add is not None),
            out_specs=[whole, small],
        ),
        out_shape=[shaped((tokens, model), BF16), shaped((experts, model), F32)],
        compiler_params=params(),
        cost_estimate=cost(
            2 * local * slots * model * tokens, 2 * model * (local * slots + 3 * tokens)
        ),
        name="combine_back",
    )(place, slot_cols, *rows, *dchosen, probs, router_rows, x, *(() if add is None else (add,)))


def per_device(
    block_in, cotangent, route_ids, gain_attn, w_qkv, w_out_attn, gain_moe, router, w_in, w_out
):
    n_dp, n_heads, n_exp = (lax.axis_size(name) for name in ("dp", "heads", "expert"))
    n_z = n_dp // CORES
    dp, head, exp = (lax.axis_index(name) for name in ("dp", "heads", "expert"))
    z, core = dp // CORES, dp % CORES
    low = core == 0
    images, seq, half_width = block_in.shape
    span = -(-seq // 16) * 16
    rows = images * span
    model = half_width * n_heads
    width = w_qkv.shape[2]
    shard = w_qkv.shape[0]
    expert_count = router.shape[1]
    group = w_in.shape[1]
    local = group // CORES
    part_rows, _, hidden_width = w_in.shape
    capacity = 20 * images * seq // (7 * expert_count)
    slots = -(-capacity // 16) * 16
    blocks = n_exp * CORES
    rest = 128

    def shift(value, axis, step):
        size = lax.axis_size(axis)
        return lax.ppermute(value, axis, [(i, (i + step) % size) for i in range(size)])

    def shift_z(value, step):
        pairs = [
            (a * CORES + c, ((a + step) % n_z) * CORES + c) for a in range(n_z) for c in range(CORES)
        ]
        return lax.ppermute(value, "dp", pairs)

    def swap_core(value):
        return lax.ppermute(value, "dp", [(i, i ^ 1) for i in range(n_dp)])

    def place_at(pieces, index, count):
        if count == 2:
            first = index == 0
            return jnp.stack(
                [jnp.where(first, pieces[0], pieces[1]), jnp.where(first, pieces[1], pieces[0])]
            )
        out = jnp.zeros((count,) + pieces[0].shape, pieces[0].dtype)
        for k, piece in enumerate(pieces):
            out = lax.dynamic_update_index_in_dim(out, piece, (index - k) % count, 0)
        return out

    def spread(value, axis):
        return [value] + [shift(value, axis, k) for k in range(1, lax.axis_size(axis))]

    def take(value, index, dim=0):
        return lax.dynamic_index_in_dim(value, index, dim, keepdims=False)

    def expert_shards():
        both = jnp.stack([w_out, w_in]).reshape(2, part_rows, CORES, local, hidden_width)
        by_core = both.transpose(2, 3, 0, 1, 4)
        other = swap_core(take(by_core, 1 - core))
        mine = take(by_core, core)
        return jnp.concatenate(
            [jnp.where(low, mine, other), jnp.where(low, other, mine)], axis=2
        )

    ways_up = n_z // 2
    ways_down = n_z - 1 - ways_up

    def ring(piece):
        pieces = [piece] + [None] * (n_z - 1)
        for k in range(1, ways_up + 1):
            pieces[k] = shift_z(pieces[k - 1], 1)
        for k in range(1, ways_down + 1):
            pieces[n_z - k] = shift_z(pieces[(n_z - k + 1) % n_z], -1)
        return pieces

    def blocks_of(value, hold=()):
        along = spread(value, "expert")
        along = along[:1] + [after(part, *hold) for part in along[1:]]
        return along + [swap_core(part) for part in along]

    tail = jnp.concatenate(
        [router, gain_attn[:, None], gain_moe[:, None],
         jnp.zeros((shard, rest - expert_count - 2), BF16)], axis=1
    )
    own_pack = jnp.concatenate([w_qkv.reshape(shard, 3 * width), w_out_attn, tail], axis=1)
    columns = own_pack.shape[1]
    shards = expert_shards()
    ids = jnp.pad(route_ids, ((0, 0), (0, span - seq), (0, 0)), constant_values=-1)
    ids_all = jnp.stack(blocks_of(ids.reshape(rows, 2).T))
    pack_z = place_at(
        [own_pack] + [after(shift_z(own_pack, k), shards) for k in range(1, n_z)], z, n_z
    )
    pack = place_at(spread(after(pack_z, ids_all), "expert"), exp, n_exp)
    pieces = []
    for e in range(local):
        pieces.append(ring(after(shards[e], pieces[-1][1]) if e else shards[e]))
    last = local - 1

    other_pack = swap_core(pack)
    pack = jnp.stack([jnp.where(low, pack, other_pack), jnp.where(low, other_pack, pack)])
    pack = pack.transpose(2, 0, 1, 3, 4).reshape(model, columns)
    side = pack[:, 4 * width :].T
    router_rows = side[:expert_count]
    gain_one = side[expert_count : expert_count + 1].astype(F32)
    gain_two = side[expert_count + 1 : expert_count + 2].astype(F32)

    def full_rows(value):
        padded = jnp.pad(value, ((0, 0), (0, span - seq), (0, 0))).reshape(rows, half_width)
        parts = place_at(spread(padded, "heads"), head, n_heads)
        return jnp.concatenate([parts[i] for i in range(n_heads)], axis=-1)

    inputs = full_rows(block_in)

    first_expert = exp * group + core * local
    named = first_expert + jnp.arange(local, dtype=jnp.int32)
    chosen = jnp.any(ids_all[:, None, :, :] == named[None, :, None, None], axis=2)
    before = (jnp.arange(rows)[:, None] < jnp.arange(rows)[None, :]).astype(BF16)
    rank = jnp.dot(
        chosen.astype(BF16).reshape(blocks * local, rows), before, preferred_element_type=F32
    ).astype(jnp.int32).reshape(blocks, local, rows)
    slot_of = jnp.where(chosen, rank, -1)
    slot_cols = slot_of.transpose(0, 2, 1)
    place = [jnp.stack([z, first_expert + e]).astype(jnp.int32) for e in range(local)]

    grad_full = full_rows(cotangent)
    grads_all = blocks_of(grad_full)
    inputs_ready = after(inputs, pieces[0][1], grad_full)
    part, qkv, ctx = attend(inputs_ready, gain_one, pack, width, images, seq)
    part = after(part, pieces[0][-1])
    part_other = shift(part, "heads", 1)
    for k in range(2, n_heads):
        part_other = part_other + shift(part, "heads", k)
    part_other = after(part_other, pieces[0][ways_up])
    middle = inputs.astype(F32) + (part.astype(F32) + part_other.astype(F32))
    unit_two, scale_two = norm_parts(middle)
    normed_two = (unit_two * gain_two).astype(BF16)
    tokens_all = blocks_of(normed_two, (pieces[last][1],))

    done = []

    def begin_rings(e, *hold):
        rows_e, mids_e = done[e][:2]
        rings.append(weight_grad(place[e], after(rows_e, *hold), mids_e, n_z))

    def ring_first(e):
        return shift_z(rings[e][-ways_up % n_z], 1)

    def ring_down(e):
        chunks = rings[e]
        downward = chunks[ways_down]
        for k in range(ways_down - 1, 0, -1):
            downward = (shift_z(downward, -1).astype(F32) + chunks[k].astype(F32)).astype(BF16)
        return shift_z(downward, -1)

    def ring_middle(e, upward, *hold):
        chunks = rings[e]
        for k in range(ways_up - 1, 0, -1):
            own = after(chunks[n_z - k], *hold)
            upward = (upward.astype(F32) + own.astype(F32)).astype(BF16)
            if k > 1:
                upward = shift_z(upward, 1)
        return upward

    def ring_end(e, upward, downward, *hold):
        own = after(rings[e][0], *hold).astype(F32)
        return own + shift_z(upward, 1).astype(F32) + downward.astype(F32)

    rings = []
    for e in range(local):
        here = list(pieces[e])
        if e:
            here[0] = after(here[0], rings[-1][0])
        done.append(
            run_expert(
                place[e], slot_of[:, e : e + 1, :], router_rows, tokens_all, grads_all, here, slots
            )
        )
        if e < local - 1:
            begin_rings(e)
    drows, yrows, dchosen = ([r[i] for r in done] for i in (3, 4, 2))
    probs = done[0][5]

    arrived_zero, down_zero = ring_first(0), ring_down(0)
    drows[0] = after(drows[0], arrived_zero, down_zero)

    def back_of(b, add=None):
        return combine_back(
            place[0], slot_cols, drows, dchosen, probs, router_rows, tokens_all[b], b, add
        )

    drouter = jnp.zeros((expert_count, model), F32)
    arrived = [None] * n_exp
    for k in reversed(range(n_exp)):
        sent, more = back_of(n_exp + k)
        arrived[k] = swap_core(sent)
        drouter = drouter + more
    from_exp = []
    for k in reversed(range(n_exp)):
        total, more = back_of(k, arrived[k])
        drouter = drouter + more
        if k:
            from_exp.append(shift(total, "expert", -k))
            if k == 1:
                begin_rings(last, total)
                early = ring_middle(0, arrived_zero, total)
    dsum = after(total, early, rings[last][0]).astype(F32)
    for value in from_exp:
        dsum = dsum + value.astype(F32)
    dsum = dsum.astype(BF16)

    dsum_other = shift(dsum, "heads", 1)
    for k in range(2, n_heads):
        dsum_other = dsum_other + shift(dsum, "heads", k)
    ends = [ring_end(0, early, down_zero, dsum)]
    yrows[0] = after(yrows[0], ends[0])
    y_came = [swap_core(combine(slot_cols, yrows, n_exp + k)) for k in range(n_exp)]
    y_from = []
    for k in reversed(range(n_exp)):
        y_own = combine(slot_cols, yrows, k, y_came[k])
        if k:
            y_from.append(shift(y_own, "expert", -k))
    y_own = y_own.astype(F32)
    for value in y_from:
        y_own = y_own + value.astype(F32)
    y_own = y_own.astype(BF16)

    arrived_last, down_last = ring_first(last), ring_down(last)
    dsum_other = after(dsum_other, ends[0], arrived_last)
    dnormed_two = dsum.astype(F32) + dsum_other.astype(F32)
    scaled = dnormed_two * gain_two
    grad_gain_two = jnp.sum(dnormed_two * unit_two, axis=0)
    dmiddle = grad_full.astype(F32) + scale_two * (
        scaled
        - jnp.mean(scaled, axis=-1, keepdims=True)
        - unit_two * jnp.mean(scaled * unit_two, axis=-1, keepdims=True)
    )
    late = ring_middle(last, arrived_last, dsum_other)
    datt = after(dmiddle.astype(BF16), late)

    dside = jnp.concatenate(
        [drouter, jnp.zeros((1, model), F32), grad_gain_two[None, :],
         jnp.zeros((rest - expert_count - 2, model), F32)], axis=0
    ).T
    dnorm, stats, dpack = attend_back(
        inputs, gain_one, datt, qkv, ctx, pack, dside, expert_count, width, images, seq, n_heads
    )
    dpack = after(dpack, y_own, down_last)

    dpack = dpack.reshape(n_z, CORES, n_exp, shard, columns)
    dsent = swap_core(take(dpack, 1 - core, 1))
    dpack = (take(dpack, core, 1).astype(F32) + dsent.astype(F32)).astype(BF16)
    dtotal = take(dpack, exp, 1).astype(F32)
    for k in range(1, n_exp):
        dtotal = dtotal + shift(take(dpack, (exp + k) % n_exp, 1), "expert", k).astype(F32)
    dpack = dtotal.astype(BF16)
    ends.append(ring_end(last, late, down_last, dpack))
    dtotal = take(dpack, z).astype(F32)
    for k in range(1, n_z):
        dtotal = dtotal + shift_z(take(dpack, (z + k) % n_z), k).astype(F32)
    dside = dtotal[:, 4 * width :]
    over_heads = dside[:, : expert_count + 1].T
    summed = over_heads
    for k in range(1, n_heads):
        summed = summed + shift(over_heads, "heads", k)

    def own_half(value):
        return lax.dynamic_slice_in_dim(value, head * half_width, half_width, 1)

    def cut(value):
        return value.astype(BF16).reshape(images, span, half_width)[:, :seq]

    dn_own = take(dnorm, head).astype(F32)
    sums = stats[:, :2].T
    sums_total = sums
    for k in range(1, n_heads):
        dn_own = dn_own + shift(take(dnorm, (head + k) % n_heads), "heads", k).astype(F32)
        sums_total = sums_total + shift(sums, "heads", k)
    unit_one, scale_one = norm_parts(inputs.astype(F32))
    grad_in = own_half(dmiddle) + scale_one * (
        dn_own * own_half(gain_one)
        - sums_total[0][:, None] / model
        - own_half(unit_one) * (sums_total[1][:, None] / model)
    )

    y_total = own_half(y_own).astype(F32)
    for k in range(1, n_heads):
        there = (head + k) % n_heads
        part_y = lax.dynamic_slice_in_dim(y_own, there * half_width, half_width, 1)
        y_total = y_total + shift(part_y, "heads", k).astype(F32)
    block_out = own_half(middle) + y_total

    stacked = jnp.stack(ends).reshape(local, 2, CORES, part_rows, hidden_width)
    other = swap_core(take(stacked, 1 - core, 2).astype(BF16)).astype(F32)
    own = take(stacked, core, 2)
    joined = jnp.concatenate([jnp.where(low, own, other), jnp.where(low, other, own)], axis=0)
    grads = joined.transpose(1, 2, 0, 3)

    return (
        cut(block_out),
        cut(grad_in),
        summed[expert_count],
        dtotal[:, : 3 * width].reshape(shard, 3, width),
        dtotal[:, 3 * width : 4 * width],
        dside[:, expert_count + 1],
        summed[:expert_count].T,
        grads[1],
        grads[0],
    )


def solution(mesh):
    return jax.shard_map(
        per_device,
        mesh=mesh,
        in_specs=(
            P(("dp", "expert"), None, "heads"),
            P(("dp", "expert"), None, "heads"),
            P(("dp", "expert"), None, None),
            P(("dp", "expert")),
            P(("dp", "expert"), None, "heads"),
            P(("dp", "expert"), "heads"),
            P(("dp", "expert")),
            P(("dp", "expert"), None),
            P("dp", "expert", "heads"),
            P("dp", "expert", "heads"),
        ),
        out_specs=(
            P(("dp", "expert"), None, "heads"),
            P(("dp", "expert"), None, "heads"),
            P(("dp", "expert")),
            P(("dp", "expert"), None, "heads"),
            P(("dp", "expert"), "heads"),
            P(("dp", "expert")),
            P(("dp", "expert"), None),
            P("dp", "expert", "heads"),
            P("dp", "expert", "heads"),
        ),
        check_vma=False,
    )
```

profile of v0, /device:TPU:0, one launch (start us, length us, event | category | flops | bytes accessed | tf_op | source)
XLA Modules:
  0.0 504.2 jit_solution(16442240521356691626)
XLA Ops:
  24.4 7.2 %collective-permute-done.5 = bf16[48,1664]{1,0:T(8,128)(2,1)} collective-permute-done((bf16[48,1664]{1,0:T(8,128)(2,1)}, bf16[48,1664]{1,0:T(8,128)(2,1)}, u32[]{:S(2)}, u32[]{:S(2)}) %collective-permute-start.5) | collective-permute-done | bytes 159776 | tf_op jit(solution)/shard_map/ppermute | solution.py:473
  37.7 14.0 %collective-permute-done.10 = bf16[4,48,1664]{2,1,0:T(8,128)(2,1)} collective-permute-done((bf16[4,48,1664]{2,1,0:T(8,128)(2,1)}, bf16[4,48,1664]{2,1,0:T(8,128)(2,1)}, u32[]{:S(2)}, u32[]{:S(2)}) %collective-permute-start.10) | collective-permute-done | bytes 639008 | tf_op jit(solution)/shard_map/ppermute | solution.py:467
  62.3 12.1 %collective-permute-done = bf16[832,384]{1,0:T(8,128)(2,1)} collective-permute-done((bf16[832,384]{1,0:T(8,128)(2,1)}, bf16[832,384]{1,0:T(8,128)(2,1)}, u32[]{:S(2)}, u32[]{:S(2)}) %collective-permute-start) | collective-permute-done | bytes 639008 | tf_op jit(solution)/shard_map/ppermute | solution.py:467
  80.2 7.1 %collective-permute-done.2.refs_9_.refs_13_ = bf16[2,192,1536]{2,1,0:T(8,128)(2,1)S(1)} collective-permute-done((bf16[2,192,1536]{2,1,0:T(8,128)(2,1)}, bf16[2,192,1536]{2,1,0:T(8,128)(2,1)S(1)}, u32[]{:S(2)}, u32[]{:S(2)}) %collective-permute-start.2) | collective-permute-done | bytes 1179680 | tf_op jit(solution)/shard_map/ppermute | solution.py:473
  92.4 10.9 %attend.1 = (bf16[832,768]{1,0:T(8,128)(2,1)}, bf16[832,1152]{1,0:T(8,128)(2,1)}, bf16[832,384]{1,0:T(8,128)(2,1)}) custom-call(bf16[832,768]{1,0:T(8,128)(2,1)} %pad_maximum_fusion.2.x_ref, f32[1,768]{1,0:T(1,128)} %copy.214.gain_ref, bf16[768,1664]{1,0:T(8,128)(2,1)} %bitcast.146, bf16[768,1664]{1,0:T(8,128)(2,1)} %bitcast.147), custom_call_target="tpu_custom_call" | custom-call | flops 38338560 | bytes 79872 | tf_op jit(solution)/shard_map/attend/pallas_call | solution.py:88
  103.3 8.4 %collective-permute-done.12.refs_11_.refs_15_ = bf16[2,192,1536]{2,1,0:T(8,128)(2,1)} collective-permute-done((bf16[2,192,1536]{2,1,0:T(8,128)(2,1)}, bf16[2,192,1536]{2,1,0:T(8,128)(2,1)}, u32[]{:S(2)}, u32[]{:S(2)}) %collective-permute-start.12) | collective-permute-done | bytes 1179680 | tf_op jit(solution)/shard_map/ppermute | solution.py:473
  113.2 14.8 %collective-permute-start.14 = (bf16[2,192,1536]{2,1,0:T(8,128)(2,1)S(1)}, bf16[2,192,1536]{2,1,0:T(8,128)(2,1)S(1)}, u32[]{:S(2)}, u32[]{:S(2)}) collective-permute-start(bf16[2,192,1536]{2,1,0:T(8,128)(2,1)S(1)} %copy-done.21), channel_id=1, source_target_pairs={{0,8},{4,12},{8,16},{12,20},{16,24},{20,28},{24,0},{28,4},{1,9},{5... | collective-permute-start | bytes 3538952 | tf_op jit(solution)/shard_map/ppermute | solution.py:473
  128.9 13.6 %collective-permute-done.14.refs_10_.refs_14_ = bf16[2,192,1536]{2,1,0:T(8,128)(2,1)S(1)} collective-permute-done((bf16[2,192,1536]{2,1,0:T(8,128)(2,1)S(1)}, bf16[2,192,1536]{2,1,0:T(8,128)(2,1)S(1)}, u32[]{:S(2)}, u32[]{:S(2)}) %collective-permute-start.14) | collective-permute-done | bytes 1179680 | tf_op jit(solution)/shard_map/ppermute | solution.py:473
  148.5 10.6 %collective-permute-start.16 = (bf16[2,192,1536]{2,1,0:T(8,128)(2,1)S(1)}, bf16[2,192,1536]{2,1,0:T(8,128)(2,1)S(1)}, u32[]{:S(2)}, u32[]{:S(2)}) collective-permute-start(bf16[2,192,1536]{2,1,0:T(8,128)(2,1)S(1)} %copy-done.8), channel_id=1, source_target_pairs={{0,8},{4,12},{8,16},{12,20},{16,24},{20,28},{24,0},{28,4},{1,9},{5... | collective-permute-start | bytes 3538952 | tf_op jit(solution)/shard_map/ppermute | solution.py:473
  159.6 17.3 %collective-permute-done.16.refs_9_.refs_13_ = bf16[2,192,1536]{2,1,0:T(8,128)(2,1)S(1)} collective-permute-done((bf16[2,192,1536]{2,1,0:T(8,128)(2,1)S(1)}, bf16[2,192,1536]{2,1,0:T(8,128)(2,1)S(1)}, u32[]{:S(2)}, u32[]{:S(2)}) %collective-permute-start.16) | collective-permute-done | bytes 1179680 | tf_op jit(solution)/shard_map/ppermute | solution.py:473
  191.1 28.9 %expert.2 = (bf16[2,4,288,768]{3,2,1,0:T(8,128)(2,1)}, bf16[2,4,288,1536]{3,2,1,0:T(8,128)(2,1)}, f32[4,1,832]{2,1,0:T(1,128)}, bf16[4,288,768]{2,1,0:T(8,128)(2...) custom-call(s32[2]{0:T(128)} %pad_add_fusion.1.place_ref, s32[4,1,832]{2,1,0:T(1,128)} %copy.219.slot_ref, ...), custom_call_target="tpu_custom_call" | custom-call | flops 215875584 | bytes 221184 | tf_op jit(solution)/shard_map/expert/pallas_call | solution.py:289
  220.0 12.0 %weight_grad.2 = (bf16[2,192,1536]{2,1,0:T(8,128)(2,1)}, bf16[2,192,1536]{2,1,0:T(8,128)(2,1)}, bf16[2,192,1536]{2,1,0:T(8,128)(2,1)}, bf16[2,192,1536]{2,1,0:T(8,128)(2,1)}) custom-call(s32[2]{0:T(128)} %pad_add_fusion.1.place_ref, bf16[2,4,288,768]{3,2,1,0:T(8,128)(2,1)} %get-tuple-element.74.rows_ref, bf16[2,4,288,1536]{3,2,1,0:T(8,128)(2,1)} %get-tuple-element.75.cols_ref), custom_call_target="tpu_custom_call" | custom-call | flops 84934656 | bytes 239616 | tf_op jit(solution)/shard_map/weight_grad/pallas_call | solution.py:337
  238.0 29.3 %collective-permute-done.25.refs_11_.refs_15_ = bf16[2,192,1536]{2,1,0:T(8,128)(2,1)} collective-permute-done((bf16[2,192,1536]{2,1,0:T(8,128)(2,1)}, bf16[2,192,1536]{2,1,0:T(8,128)(2,1)}, u32[]{:S(2)}, u32[]{:S(2)}) %collective-permute-start.25) | collective-permute-done | bytes 1179680 | tf_op jit(solution)/shard_map/ppermute | solution.py:473
  267.3 29.0 %expert.3 = (bf16[2,4,288,768]{3,2,1,0:T(8,128)(2,1)}, bf16[2,4,288,1536]{3,2,1,0:T(8,128)(2,1)}, f32[4,1,832]{2,1,0:T(1,128)}, bf16[4,288,768]{2,1,0:T(8,128)(2...) custom-call(s32[2]{0:T(128)} %pad_add_fusion.2.place_ref, s32[4,1,832]{2,1,0:T(1,128)} %copy.221.slot_ref, ...), custom_call_target="tpu_custom_call" | custom-call | flops 215875584 | bytes 221184 | tf_op jit(solution)/shard_map/expert/pallas_call | solution.py:289
  296.4 5.5 %combine_back.6 = (bf16[832,768]{1,0:T(8,128)(2,1)}, f32[8,768]{1,0:T(8,128)}) custom-call(s32[2]{0:T(128)} %pad_add_fusion.1.place_ref, s32[4,832,2]{2,1,0:T(8,128)} %bitcast.137, bf16[4,288,768]{2,1,0:T(8,128)(2,1)} %get-tuple-element.80.refs_0_, bf16[4,288,768]{2,1,0:T(8,128)(2,1)} %get-tuple-element.82.refs_1_, f32[4,1,832]{2,1,0:T(1,128)} %get-tuple-element.83.refs_2_, ...), custom_call_target="tpu_custom_call" | custom-call | flops 11501568 | bytes 73728 | tf_op jit(solution)/shard_map/combine_back/pallas_call | solution.py:421
  309.0 5.9 %combine_back.7 = (bf16[832,768]{1,0:T(8,128)(2,1)}, f32[8,768]{1,0:T(8,128)}) custom-call(s32[2]{0:T(128)} %pad_add_fusion.1.place_ref, s32[4,832,2]{2,1,0:T(8,128)} %bitcast.139, bf16[4,288,768]{2,1,0:T(8,128)(2,1)} %get-tuple-element.80.refs_0_, bf16[4,288,768]{2,1,0:T(8,128)(2,1)} %get-tuple-element.82.refs_1_, f32[4,1,832]{2,1,0:T(1,128)} %get-tuple-element.83.refs_2_, ...), custom_call_target="tpu_custom_call" | custom-call | flops 11501568 | bytes 73728 | tf_op jit(solution)/shard_map/combine_back/pallas_call | solution.py:421
  316.3 5.8 %combine_back.5 = (bf16[832,768]{1,0:T(8,128)(2,1)}, f32[8,768]{1,0:T(8,128)}) custom-call(s32[2]{0:T(128)} %pad_add_fusion.1.place_ref, s32[4,832,2]{2,1,0:T(8,128)} %bitcast.140, bf16[4,288,768]{2,1,0:T(8,128)(2,1)} %get-tuple-element.80.refs_0_, bf16[4,288,768]{2,1,0:T(8,128)(2,1)} %get-tuple-element.82.refs_1_, f32[4,1,832]{2,1,0:T(1,128)} %get-tuple-element.83.refs_2_, ...), custom_call_target="tpu_custom_call" | custom-call | flops 11501568 | bytes 73728 | tf_op jit(solution)/shard_map/combine_back/pallas_call | solution.py:421
  322.1 12.2 %weight_grad.3 = (bf16[2,192,1536]{2,1,0:T(8,128)(2,1)}, bf16[2,192,1536]{2,1,0:T(8,128)(2,1)}, bf16[2,192,1536]{2,1,0:T(8,128)(2,1)}, bf16[2,192,1536]{2,1,0:T(8,128)(2,1)}) custom-call(s32[2]{0:T(128)} %pad_add_fusion.2.place_ref, bf16[2,4,288,768]{3,2,1,0:T(8,128)(2,1)} %get-tuple-element.93.rows_ref, bf16[2,4,288,1536]{3,2,1,0:T(8,128)(2,1)} %get-tuple-element.94.cols_ref), custom_call_target="tpu_custom_call" | custom-call | flops 84934656 | bytes 239616 | tf_op jit(solution)/shard_map/weight_grad/pallas_call | solution.py:337
  334.3 10.7 %collective-permute-done.28 = bf16[832,768]{1,0:T(8,128)(2,1)S(1)} collective-permute-done((bf16[832,768]{1,0:T(8,128)(2,1)}, bf16[832,768]{1,0:T(8,128)(2,1)S(1)}, u32[]{:S(2)}, u32[]{:S(2)}) %collective-permute-start.28) | collective-permute-done | bytes 1277984 | tf_op jit(solution)/shard_map/ppermute | solution.py:467
  367.0 18.0 %collective-permute-done.35 = bf16[2,192,1536]{2,1,0:T(8,128)(2,1)} collective-permute-done((bf16[2,192,1536]{2,1,0:T(8,128)(2,1)}, bf16[2,192,1536]{2,1,0:T(8,128)(2,1)}, u32[]{:S(2)}, u32[]{:S(2)}) %collective-permute-start.35) | collective-permute-done | bytes 1179680 | tf_op jit(solution)/shard_map/ppermute | solution.py:473
  401.3 20.5 %attend_back.1 = (bf16[2,832,384]{2,1,0:T(8,128)(2,1)}, f32[832,128]{1,0:T(8,128)}, bf16[768,1664]{1,0:T(8,128)(2,1)}) custom-call(bf16[832,768]{1,0:T(8,128)(2,1)} %pad_maximum_fusion.2.x_ref, f32[1,768]{1,0:T(1,128)} %copy.214.gain_ref, bf16[832,768]{1,0:T(8,128)(2,1)} %get-tuple-element.104.datt_ref, bf16[832,1152]{1,0:T(8,128)(2,1)} %get-tuple-element.105.qkv_ref, ...), custom_call_target="tpu_custom_call" | custom-call | flops 107347968 | bytes 119808 | tf_op jit(solution)/shard_map/attend_back/pallas_call | solution.py:179
  439.4 13.2 %collective-permute-done.36 = bf16[832,384]{1,0:T(8,128)(2,1)S(1)} collective-permute-done((bf16[832,384]{1,0:T(8,128)(2,1)S(1)}, bf16[832,384]{1,0:T(8,128)(2,1)S(1)}, u32[]{:S(2)}, u32[]{:S(2)}) %collective-permute-start.36) | collective-permute-done | bytes 639008 | tf_op jit(solution)/shard_map/ppermute | solution.py:467
  452.6 13.3 %collective-permute-done.33 = bf16[832,384]{1,0:T(8,128)(2,1)S(1)} collective-permute-done((bf16[832,384]{1,0:T(8,128)(2,1)S(1)}, bf16[832,384]{1,0:T(8,128)(2,1)S(1)}, u32[]{:S(2)}, u32[]{:S(2)}) %collective-permute-start.33) | collective-permute-done | bytes 639008 | tf_op jit(solution)/shard_map/ppermute | solution.py:467
  478.6 8.3 %collective-permute-done.42 = bf16[48,1664]{1,0:T(8,128)(2,1)S(1)} collective-permute-done((bf16[48,1664]{1,0:T(8,128)(2,1)S(1)}, bf16[48,1664]{1,0:T(8,128)(2,1)S(1)}, u32[]{:S(2)}, u32[]{:S(2)}) %collective-permute-start.42) | collective-permute-done | bytes 159776 | tf_op jit(solution)/shard_map/ppermute | solution.py:473
  (291 shorter events, 173.5 us)
Async XLA Ops:
  54.3 33.1 %collective-permute-start.11 = (bf16[2,4,48,1664]{3,2,0,1:T(8,128)(2,1)}, bf16[2,4,48,1664]{3,2,0,1:T(8,128)(2,1)}, u32[]{:S(2)}, u32[]{:S(2)}) collective-permute-start(bf16[2,4,48,1664]{3,2,0,1:T(8,128)(2,1)} %pad_maximum_fusion.4), channel_id=1, source_target_pairs={{0,4},{4,0},{8,12},{12,8},{16,20},{20,16},{24,28},{28,24},{1,5},{5... | collective-permute-start | bytes 3833864 | tf_op jit(solution)/shard_map/ppermute | solution.py:476
  56.4 30.9 %collective-permute-start.2 = (bf16[2,192,1536]{2,1,0:T(8,128)(2,1)}, bf16[2,192,1536]{2,1,0:T(8,128)(2,1)S(1)}, u32[]{:S(2)}, u32[]{:S(2)}) collective-permute-start(bf16[2,192,1536]{2,1,0:T(8,128)(2,1)} %get-tuple-element.189.refs_8_.refs_12_), channel_id=1, source_target_pairs={{0,8},{4,12},{8,16},{12,20},{16,24},{20,28},{24,0},{28,4},{1,9},{5... | collective-permute-start | bytes 3538952 | tf_op jit(solution)/shard_map/ppermute | solution.py:473
  77.1 34.6 %collective-permute-start.12 = (bf16[2,192,1536]{2,1,0:T(8,128)(2,1)}, bf16[2,192,1536]{2,1,0:T(8,128)(2,1)}, u32[]{:S(2)}, u32[]{:S(2)}) collective-permute-start(bf16[2,192,1536]{2,1,0:T(8,128)(2,1)} %get-tuple-element.189.refs_8_.refs_12_), channel_id=1, source_target_pairs={{0,24},{4,28},{8,0},{12,4},{16,8},{20,12},{24,16},{28,20},{1,25},{... | collective-permute-start | bytes 3538952 | tf_op jit(solution)/shard_map/ppermute | solution.py:473
  111.7 31.9 %collective-permute-start.13 = (bf16[832,768]{1,0:T(8,128)(2,1)}, bf16[832,768]{1,0:T(8,128)(2,1)S(1)}, u32[]{:S(2)}, u32[]{:S(2)}) collective-permute-start(bf16[832,768]{1,0:T(8,128)(2,1)} %get-tuple-element.69), channel_id=1, source_target_pairs={{0,2},{2,0},{1,3},{3,1},{4,6},{6,4},{5,7},{7,5},{8,10},{10,8},{9,1... | collective-permute-start | bytes 3833864 | tf_op jit(solution)/shard_map/ppermute | solution.py:467
  113.2 29.4 %collective-permute-start.14 = (bf16[2,192,1536]{2,1,0:T(8,128)(2,1)S(1)}, bf16[2,192,1536]{2,1,0:T(8,128)(2,1)S(1)}, u32[]{:S(2)}, u32[]{:S(2)}) collective-permute-start(bf16[2,192,1536]{2,1,0:T(8,128)(2,1)S(1)} %copy-done.21), channel_id=1, source_target_pairs={{0,8},{4,12},{8,16},{12,20},{16,24},{20,28},{24,0},{28,4},{1,9},{5... | collective-permute-start | bytes 3538952 | tf_op jit(solution)/shard_map/ppermute | solution.py:473
  127.9 31.2 %collective-permute-start.19 = (bf16[832,768]{1,0:T(8,128)(2,1)}, bf16[832,768]{1,0:T(8,128)(2,1)}, u32[]{:S(2)}, u32[]{:S(2)}) collective-permute-start(bf16[832,768]{1,0:T(8,128)(2,1)} %pad_maximum_fusion.3.refs_4_), channel_id=1, source_target_pairs={{0,1},{1,0},{2,3},{3,2},{4,5},{5,4},{6,7},{7,6},{8,9},{9,8},{10,11... | collective-permute-start | bytes 3833864 | tf_op jit(solution)/shard_map/ppermute | solution.py:467
  147.6 29.4 %collective-permute-start.15 = (bf16[832,768]{1,0:T(8,128)(2,1)S(1)}, bf16[832,768]{1,0:T(8,128)(2,1)S(1)}, u32[]{:S(2)}, u32[]{:S(2)}) collective-permute-start(bf16[832,768]{1,0:T(8,128)(2,1)S(1)} %multiply_convert_fusion.refs_0_.refs_6_), channel_id=1, source_target_pairs={{0,1},{1,0},{2,3},{3,2},{4,5},{5,4},{6,7},{7,6},{8,9},{9,8},{10,11... | collective-permute-start | bytes 3833864 | tf_op jit(solution)/shard_map/ppermute | solution.py:467
  159.1 29.7 %collective-permute-start.20 = (bf16[832,768]{1,0:T(8,128)(2,1)}, bf16[832,768]{1,0:T(8,128)(2,1)}, u32[]{:S(2)}, u32[]{:S(2)}) collective-permute-start(bf16[832,768]{1,0:T(8,128)(2,1)} %pad_maximum_fusion.3.refs_4_), channel_id=1, source_target_pairs={{0,4},{4,0},{8,12},{12,8},{16,20},{20,16},{24,28},{28,24},{1,5},{5... | collective-permute-start | bytes 3833864 | tf_op jit(solution)/shard_map/ppermute | solution.py:476
  159.1 31.9 %collective-permute-start.21 = (bf16[832,768]{1,0:T(8,128)(2,1)}, bf16[832,768]{1,0:T(8,128)(2,1)}, u32[]{:S(2)}, u32[]{:S(2)}) collective-permute-start(bf16[832,768]{1,0:T(8,128)(2,1)} %collective-permute-done.19.refs_5_), channel_id=1, source_target_pairs={{0,4},{4,0},{8,12},{12,8},{16,20},{20,16},{24,28},{28,24},{1,5},{5... | collective-permute-start | bytes 3833864 | tf_op jit(solution)/shard_map/ppermute | solution.py:476
  159.6 31.4 %collective-permute-start.17 = (bf16[832,768]{1,0:T(8,128)(2,1)S(1)}, bf16[832,768]{1,0:T(8,128)(2,1)}, u32[]{:S(2)}, u32[]{:S(2)}) collective-permute-start(bf16[832,768]{1,0:T(8,128)(2,1)S(1)} %multiply_convert_fusion.refs_0_.refs_6_), channel_id=1, source_target_pairs={{0,4},{4,0},{8,12},{12,8},{16,20},{20,16},{24,28},{28,24},{1,5},{5... | collective-permute-start | bytes 3833864 | tf_op jit(solution)/shard_map/ppermute | solution.py:476
  188.1 79.2 %collective-permute-start.25 = (bf16[2,192,1536]{2,1,0:T(8,128)(2,1)}, bf16[2,192,1536]{2,1,0:T(8,128)(2,1)}, u32[]{:S(2)}, u32[]{:S(2)}) collective-permute-start(bf16[2,192,1536]{2,1,0:T(8,128)(2,1)} %get-tuple-element.81.refs_8_.refs_12_), channel_id=1, source_target_pairs={{0,24},{4,28},{8,0},{12,4},{16,8},{20,12},{24,16},{28,20},{1,25},{... | collective-permute-start | bytes 3538952 | tf_op jit(solution)/shard_map/ppermute | solution.py:473
  188.9 78.5 %collective-permute-start.24 = (bf16[2,192,1536]{2,1,0:T(8,128)(2,1)}, bf16[2,192,1536]{2,1,0:T(8,128)(2,1)}, u32[]{:S(2)}, u32[]{:S(2)}) collective-permute-start(bf16[2,192,1536]{2,1,0:T(8,128)(2,1)} %copy-done.22), channel_id=1, source_target_pairs={{0,8},{4,12},{8,16},{12,20},{16,24},{20,28},{24,0},{28,4},{1,9},{5... | collective-permute-start | bytes 3538952 | tf_op jit(solution)/shard_map/ppermute | solution.py:473
  232.0 64.3 %collective-permute-start.22 = (bf16[2,192,1536]{2,1,0:T(8,128)(2,1)}, bf16[2,192,1536]{2,1,0:T(8,128)(2,1)S(1)}, u32[]{:S(2)}, u32[]{:S(2)}) collective-permute-start(bf16[2,192,1536]{2,1,0:T(8,128)(2,1)} %get-tuple-element.78), channel_id=1, source_target_pairs={{0,8},{4,12},{8,16},{12,20},{16,24},{20,28},{24,0},{28,4},{1,9},{5... | collective-permute-start | bytes 3538952 | tf_op jit(solution)/shard_map/ppermute | solution.py:473
  232.1 64.3 %collective-permute-start.23 = (bf16[2,192,1536]{2,1,0:T(8,128)(2,1)}, bf16[2,192,1536]{2,1,0:T(8,128)(2,1)}, u32[]{:S(2)}, u32[]{:S(2)}) collective-permute-start(bf16[2,192,1536]{2,1,0:T(8,128)(2,1)} %get-tuple-element.79), channel_id=1, source_target_pairs={{0,24},{4,28},{8,0},{12,4},{16,8},{20,12},{24,16},{28,20},{1,25},{... | collective-permute-start | bytes 3538952 | tf_op jit(solution)/shard_map/ppermute | solution.py:473
  314.9 30.2 %collective-permute-start.28 = (bf16[832,768]{1,0:T(8,128)(2,1)}, bf16[832,768]{1,0:T(8,128)(2,1)S(1)}, u32[]{:S(2)}, u32[]{:S(2)}) collective-permute-start(bf16[832,768]{1,0:T(8,128)(2,1)} %get-tuple-element.90), channel_id=1, source_target_pairs={{0,1},{1,0},{2,3},{3,2},{4,5},{5,4},{6,7},{7,6},{8,9},{9,8},{10,11... | collective-permute-start | bytes 3833864 | tf_op jit(solution)/shard_map/ppermute | solution.py:467
  315.1 31.4 %collective-permute-start.29 = (bf16[2,192,1536]{2,1,0:T(8,128)(2,1)S(1)}, bf16[2,192,1536]{2,1,0:T(8,128)(2,1)S(1)}, u32[]{:S(2)}, u32[]{:S(2)}) collective-permute-start(bf16[2,192,1536]{2,1,0:T(8,128)(2,1)S(1)} %add_convert_fusion.3), channel_id=1, source_target_pairs={{0,8},{4,12},{8,16},{12,20},{16,24},{20,28},{24,0},{28,4},{1,9},{5... | collective-permute-start | bytes 3538952 | tf_op jit(solution)/shard_map/ppermute | solution.py:473
  353.6 31.5 %collective-permute-start.34 = (bf16[832,768]{1,0:T(8,128)(2,1)}, bf16[832,768]{1,0:T(8,128)(2,1)}, u32[]{:S(2)}, u32[]{:S(2)}) collective-permute-start(bf16[832,768]{1,0:T(8,128)(2,1)} %add_convert_fusion.1), channel_id=1, source_target_pairs={{0,2},{2,0},{1,3},{3,1},{4,6},{6,4},{5,7},{7,5},{8,10},{10,8},{9,1... | collective-permute-start | bytes 3833864 | tf_op jit(solution)/shard_map/ppermute | solution.py:467
  354.1 31.0 %collective-permute-start.35 = (bf16[2,192,1536]{2,1,0:T(8,128)(2,1)}, bf16[2,192,1536]{2,1,0:T(8,128)(2,1)}, u32[]{:S(2)}, u32[]{:S(2)}) collective-permute-start(bf16[2,192,1536]{2,1,0:T(8,128)(2,1)} %get-tuple-element.100), channel_id=1, source_target_pairs={{0,8},{4,12},{8,16},{12,20},{16,24},{20,28},{24,0},{28,4},{1,9},{5... | collective-permute-start | bytes 3538952 | tf_op jit(solution)/shard_map/ppermute | solution.py:473
  354.5 70.2 %collective-permute-start.38 = (bf16[2,192,1536]{2,1,0:T(8,128)(2,1)}, bf16[2,192,1536]{2,1,0:T(8,128)(2,1)}, u32[]{:S(2)}, u32[]{:S(2)}) collective-permute-start(bf16[2,192,1536]{2,1,0:T(8,128)(2,1)} %get-tuple-element.114), channel_id=1, source_target_pairs={{0,24},{4,28},{8,0},{12,4},{16,8},{20,12},{24,16},{28,20},{1,25},{... | collective-permute-start | bytes 3538952 | tf_op jit(solution)/shard_map/ppermute | solution.py:473
  362.2 32.7 %collective-permute-start.30 = (bf16[832,768]{1,0:T(8,128)(2,1)}, bf16[832,768]{1,0:T(8,128)(2,1)S(1)}, u32[]{:S(2)}, u32[]{:S(2)}) collective-permute-start(bf16[832,768]{1,0:T(8,128)(2,1)} %combine.4), channel_id=1, source_target_pairs={{0,4},{4,0},{8,12},{12,8},{16,20},{20,16},{24,28},{28,24},{1,5},{5... | collective-permute-start | bytes 3833864 | tf_op jit(solution)/shard_map/ppermute | solution.py:476
  366.7 55.1 %collective-permute-start.32 = (bf16[832,768]{1,0:T(8,128)(2,1)}, bf16[832,768]{1,0:T(8,128)(2,1)}, u32[]{:S(2)}, u32[]{:S(2)}) collective-permute-start(bf16[832,768]{1,0:T(8,128)(2,1)} %combine.7), channel_id=1, source_target_pairs={{0,1},{1,0},{2,3},{3,2},{4,5},{5,4},{6,7},{7,6},{8,9},{9,8},{10,11... | collective-permute-start | bytes 3833864 | tf_op jit(solution)/shard_map/ppermute | solution.py:467
  426.1 47.5 %collective-permute-start.45 = (bf16[2,192,1536]{2,1,0:T(8,128)(2,1)}, bf16[2,192,1536]{2,1,0:T(8,128)(2,1)S(1)}, u32[]{:S(2)}, u32[]{:S(2)}) collective-permute-start(bf16[2,192,1536]{2,1,0:T(8,128)(2,1)} %add_convert_fusion.2), channel_id=1, source_target_pairs={{0,8},{4,12},{8,16},{12,20},{16,24},{20,28},{24,0},{28,4},{1,9},{5... | collective-permute-start | bytes 3538952 | tf_op jit(solution)/shard_map/ppermute | solution.py:473
  429.6 36.3 %collective-permute-start.33 = (bf16[832,384]{1,0:T(8,128)(2,1)S(1)}, bf16[832,384]{1,0:T(8,128)(2,1)S(1)}, u32[]{:S(2)}, u32[]{:S(2)}) collective-permute-start(bf16[832,384]{1,0:T(8,128)(2,1)S(1)} %constant_dynamic-slice_fusion), channel_id=1, source_target_pairs={{0,2},{2,0},{1,3},{3,1},{4,6},{6,4},{5,7},{7,5},{8,10},{10,8},{9,1... | collective-permute-start | bytes 1916936 | tf_op jit(solution)/shard_map/ppermute | solution.py:467
  433.4 35.5 %collective-permute-start.40 = (bf16[4,48,1664]{2,1,0:T(8,128)(2,1)S(1)}, bf16[4,48,1664]{2,1,0:T(8,128)(2,1)S(1)}, u32[]{:S(2)}, u32[]{:S(2)}) collective-permute-start(bf16[4,48,1664]{2,1,0:T(8,128)(2,1)S(1)} %dynamic-slice_bitcast_fusion.1), channel_id=1, source_target_pairs={{0,1},{1,0},{2,3},{3,2},{4,5},{5,4},{6,7},{7,6},{8,9},{9,8},{10,11... | collective-permute-start | bytes 1916936 | tf_op jit(solution)/shard_map/ppermute | solution.py:467
  (72 other events, 807.7 us)
where the time goes:
time: 514 us; the launch traced here: 504 us
  waiting for transfers between devices  180 us (35%)
  Pallas kernels  153 us (30%)
  starting transfers between devices  65.9 us (13%)
  local copies, waits for them, and re-layouts  53.1 us (10%)
  other arithmetic  50.7 us (10%)
    ppermute x18, waiting for transfers between devices, shift_z(): return lax.ppermute(value, 'dp', pairs)  111 us
    ppermute x15, waiting for transfers between devices, shift(): lax.ppermute(value, axis, [(i, (i + step) % size) for i in range(size)])  68.7 us
    pallas_call x2, Pallas kernels, run_expert(): pl.pallas_call(functools.partial(expert_kernel, depth, blocks), grid_spec...  57.9 us
    ppermute x18, starting transfers between devices, shift_z(): return lax.ppermute(value, 'dp', pairs)  48.5 us
    pallas_call x2, Pallas kernels, weight_grad(): pl.pallas_call(functools.partial(weight_grad_kernel, depth), grid_spec=pl...  24.2 us
    pallas_call x4, Pallas kernels, combine_back(): pl.pallas_call(functools.partial(combine_back_kernel, local, add is not N...  22.7 us
    pallas_call x1, Pallas kernels, attend_back(): pl.pallas_call(functools.partial(attend_back_kernel, seq, gain_at), grid=...  20.5 us
    unnamed x109, local copies, waits for them, and re-layouts  20.4 us
  transfers between devices with their start and end apart: 47, of which 17 were waited for; matrix products, arithmetic and copies ran while one was open for 15% of the time, Pallas kernels for 28%

commit v1 on v0

--- a/solution.py
+++ b/solution.py
@@ -15,6 +15,7 @@
 BF16 = jnp.bfloat16
 VMEM_LIMIT = 56 * 1024 * 1024
 SHARE = 64
+PARTS = 2
 
 
 def dot(a, b, ca, cb):
@@ -249,11 +250,17 @@
     yrows = jnp.zeros((slots, model), F32)
     tile = 512 if width % 512 == 0 else width
     curve = 0.7978845608028654
+
+    def products(start):
+        cols = slice(start, start + tile)
+        return dot(rows, win_all[:, cols], 1, 0), dot(grows, wout_all[:, cols], 1, 0)
+
+    ahead = products(0)
     for start in range(0, width, tile):
         cols = slice(start, start + tile)
-        win, wout = win_all[:, cols], wout_all[:, cols]
-        hidden = dot(rows, win, 1, 0)
-        pulled = dot(grows, wout, 1, 0)
+        hidden, pulled = ahead
+        if start + tile < width:
+            ahead = products(start + tile)
         square = hidden * hidden
         bend = jnp.tanh(hidden * (curve + curve * 0.044715 * square))
         half = 0.5 + 0.5 * bend
@@ -266,8 +273,8 @@
         dhid = (gate * pulled * slope).astype(BF16)
         mids_ref[0, 0, :, cols] = gact
         mids_ref[1, 0, :, cols] = dhid
-        drows = drows + dot(dhid, win, 1, 1)
-        yrows = yrows + dot(gact, wout, 1, 1)
+        drows = drows + dot(dhid, win_all[:, cols], 1, 1)
+        yrows = yrows + dot(gact, wout_all[:, cols], 1, 1)
     dchosen_ref[0] = jnp.sum(jnp.where(mask, dgate, 0.0), axis=0, keepdims=True)
     drows_ref[0] = drows.astype(BF16)
     yrows_ref[0] = yrows.astype(BF16)
@@ -390,8 +397,8 @@
     rows_refs, refs = refs[:local], refs[local:]
     dchosen_refs, refs = refs[:local], refs[local:]
     probs_ref, router_ref, x_ref = refs[:3]
-    out_ref, drouter_ref = refs[-2:]
-    tokens = out_ref.shape[0]
+    out_refs, drouter_ref = refs[-1 - PARTS : -1], refs[-1]
+    tokens = out_refs[0].shape[0]
     slots = rows_refs[0].shape[1]
     at = lax.broadcasted_iota(jnp.int32, (tokens, slots), 1)
     probs = probs_ref[0]
@@ -403,12 +410,15 @@
     dlogits = (probs * (dprobs - inner)).astype(BF16)
     drouter_ref[...] = dot(dlogits, x_ref[...], 1, 0)
     total = dot(dlogits, router_ref[...], 0, 0)
-    if added:
-        total = total + refs[3][...].astype(F32)
     for e in range(local):
         pick = jnp.where(at == slot_ref[0, :, e : e + 1], 1.0, 0.0).astype(BF16)
         total = total + dot(pick, rows_refs[e][0], 1, 0)
-    out_ref[...] = total.astype(BF16)
+    part = out_refs[0].shape[1]
+    for p in range(PARTS):
+        piece = total[:, p * part : (p + 1) * part]
+        if added:
+            piece = piece + refs[3 + p][...].astype(F32)
+        out_refs[p][...] = piece.astype(BF16)
 
 
 def combine_back(place, slot_cols, rows, dchosen, probs, router_rows, x, b, add=None):
@@ -416,6 +426,7 @@
     slots, model = rows[0].shape[1:]
     experts = router_rows.shape[0]
     whole = pl.BlockSpec((tokens, model), lambda i, s: (0, 0))
+    part = pl.BlockSpec((tokens, model // PARTS), lambda i, s: (0, 0))
     block = lambda *size: pl.BlockSpec((1,) + size, lambda i, s: (b, 0, 0))
     small = pl.BlockSpec((experts, model), lambda i, s: (0, 0))
     return pl.pallas_call(
@@ -427,16 +438,17 @@
             + [block(slots, model)] * local
             + [block(1, tokens)] * local
             + [block(experts, tokens), small, whole]
-            + [whole] * (add is not None),
-            out_specs=[whole, small],
-        ),
-        out_shape=[shaped((tokens, model), BF16), shaped((experts, model), F32)],
+            + [part] * (PARTS * (add is not None)),
+            out_specs=[part] * PARTS + [small],
+        ),
+        out_shape=[shaped((tokens, model // PARTS), BF16)] * PARTS
+        + [shaped((experts, model), F32)],
         compiler_params=params(),
         cost_estimate=cost(
             2 * local * slots * model * tokens, 2 * model * (local * slots + 3 * tokens)
         ),
         name="combine_back",
-    )(place, slot_cols, *rows, *dchosen, probs, router_rows, x, *(() if add is None else (add,)))
+    )(place, slot_cols, *rows, *dchosen, probs, router_rows, x, *(() if add is None else add))
 
 
 def per_device(
@@ -517,6 +529,14 @@
         along = along[:1] + [after(part, *hold) for part in along[1:]]
         return along + [swap_core(part) for part in along]
 
+    def full_rows(value):
+        padded = jnp.pad(value, ((0, 0), (0, span - seq), (0, 0))).reshape(rows, half_width)
+        parts = place_at(spread(padded, "heads"), head, n_heads)
+        return jnp.concatenate([parts[i] for i in range(n_heads)], axis=-1)
+
+    inputs = full_rows(block_in)
+    grad_full = full_rows(cotangent)
+
     tail = jnp.concatenate(
         [router, gain_attn[:, None], gain_moe[:, None],
          jnp.zeros((shard, rest - expert_count - 2), BF16)], axis=1
@@ -527,7 +547,7 @@
     ids = jnp.pad(route_ids, ((0, 0), (0, span - seq), (0, 0)), constant_values=-1)
     ids_all = jnp.stack(blocks_of(ids.reshape(rows, 2).T))
     pack_z = place_at(
-        [own_pack] + [after(shift_z(own_pack, k), shards) for k in range(1, n_z)], z, n_z
+        [own_pack] + [after(shift_z(own_pack, k), shards, inputs) for k in range(1, n_z)], z, n_z
     )
     pack = place_at(spread(after(pack_z, ids_all), "expert"), exp, n_exp)
     pieces = []
@@ -535,20 +555,14 @@
         pieces.append(ring(after(shards[e], pieces[-1][1]) if e else shards[e]))
     last = local - 1
 
-    other_pack = swap_core(pack)
+    pack = after(pack, pieces[0][1])
+    other_pack = after(swap_core(pack), grad_full)
     pack = jnp.stack([jnp.where(low, pack, other_pack), jnp.where(low, other_pack, pack)])
     pack = pack.transpose(2, 0, 1, 3, 4).reshape(model, columns)
     side = pack[:, 4 * width :].T
     router_rows = side[:expert_count]
     gain_one = side[expert_count : expert_count + 1].astype(F32)
     gain_two = side[expert_count + 1 : expert_count + 2].astype(F32)
-
-    def full_rows(value):
-        padded = jnp.pad(value, ((0, 0), (0, span - seq), (0, 0))).reshape(rows, half_width)
-        parts = place_at(spread(padded, "heads"), head, n_heads)
-        return jnp.concatenate([parts[i] for i in range(n_heads)], axis=-1)
-
-    inputs = full_rows(block_in)
 
     first_expert = exp * group + core * local
     named = first_expert + jnp.arange(local, dtype=jnp.int32)
@@ -559,17 +573,17 @@
     ).astype(jnp.int32).reshape(blocks, local, rows)
     slot_of = jnp.where(chosen, rank, -1)
     slot_cols = slot_of.transpose(0, 2, 1)
+    slot_rows = [slot_of[:, e : e + 1, :] for e in range(local)]
     place = [jnp.stack([z, first_expert + e]).astype(jnp.int32) for e in range(local)]
 
-    grad_full = full_rows(cotangent)
     grads_all = blocks_of(grad_full)
-    inputs_ready = after(inputs, pieces[0][1], grad_full)
+    inputs_ready = inputs
     part, qkv, ctx = attend(inputs_ready, gain_one, pack, width, images, seq)
     part = after(part, pieces[0][-1])
     part_other = shift(part, "heads", 1)
     for k in range(2, n_heads):
         part_other = part_other + shift(part, "heads", k)
-    part_other = after(part_other, pieces[0][ways_up])
+    part_other = after(part_other, pieces[0][ways_up], slot_cols, *slot_rows)
     middle = inputs.astype(F32) + (part.astype(F32) + part_other.astype(F32))
     unit_two, scale_two = norm_parts(middle)
     normed_two = (unit_two * gain_two).astype(BF16)
@@ -611,7 +625,7 @@
             here[0] = after(here[0], rings[-1][0])
         done.append(
             run_expert(
-                place[e], slot_of[:, e : e + 1, :], router_rows, tokens_all, grads_all, here, slots
+                place[e], slot_rows[e], router_rows, tokens_all, grads_all, here, slots
             )
         )
         if e < local - 1:
@@ -619,53 +633,52 @@
     drows, yrows, dchosen = ([r[i] for r in done] for i in (3, 4, 2))
     probs = done[0][5]
 
+    begin_rings(last)
     arrived_zero, down_zero = ring_first(0), ring_down(0)
-    drows[0] = after(drows[0], arrived_zero, down_zero)
+    early = ring_middle(0, arrived_zero)
+    arrived_last, down_last = ring_first(last), ring_down(last)
+    drows[0] = after(drows[0], early, down_zero, rings[last][0])
 
     def back_of(b, add=None):
-        return combine_back(
+        *parts, more = combine_back(
             place[0], slot_cols, drows, dchosen, probs, router_rows, tokens_all[b], b, add
         )
+        return parts, more
 
     drouter = jnp.zeros((expert_count, model), F32)
     arrived = [None] * n_exp
     for k in reversed(range(n_exp)):
         sent, more = back_of(n_exp + k)
-        arrived[k] = swap_core(sent)
+        arrived[k] = [swap_core(part) for part in sent]
         drouter = drouter + more
     from_exp = []
     for k in reversed(range(n_exp)):
         total, more = back_of(k, arrived[k])
         drouter = drouter + more
         if k:
-            from_exp.append(shift(total, "expert", -k))
-            if k == 1:
-                begin_rings(last, total)
-                early = ring_middle(0, arrived_zero, total)
-    dsum = after(total, early, rings[last][0]).astype(F32)
-    for value in from_exp:
-        dsum = dsum + value.astype(F32)
-    dsum = dsum.astype(BF16)
-
-    dsum_other = shift(dsum, "heads", 1)
-    for k in range(2, n_heads):
-        dsum_other = dsum_other + shift(dsum, "heads", k)
-    ends = [ring_end(0, early, down_zero, dsum)]
-    yrows[0] = after(yrows[0], ends[0])
+            from_exp.append([shift(part, "expert", -k) for part in total])
+    ends = [ring_end(0, early, down_zero)]
+    dsum, dsum_other = [], []
+    for p in range(PARTS):
+        value = (after(total[p], ends[0]) if p == 0 else total[p]).astype(F32)
+        for came in from_exp:
+            value = value + came[p].astype(F32)
+        dsum.append(value.astype(BF16))
+        other = shift(dsum[p], "heads", 1)
+        for k in range(2, n_heads):
+            other = other + shift(dsum[p], "heads", k)
+        dsum_other.append(other)
+    dsum_other[-1] = after(dsum_other[-1], arrived_last)
+
+    yrows[0] = after(yrows[0], dsum[-1])
     y_came = [swap_core(combine(slot_cols, yrows, n_exp + k)) for k in range(n_exp)]
-    y_from = []
-    for k in reversed(range(n_exp)):
-        y_own = combine(slot_cols, yrows, k, y_came[k])
-        if k:
-            y_from.append(shift(y_own, "expert", -k))
-    y_own = y_own.astype(F32)
-    for value in y_from:
-        y_own = y_own + value.astype(F32)
-    y_own = y_own.astype(BF16)
-
-    arrived_last, down_last = ring_first(last), ring_down(last)
-    dsum_other = after(dsum_other, ends[0], arrived_last)
-    dnormed_two = dsum.astype(F32) + dsum_other.astype(F32)
+    y_from = [
+        shift(combine(slot_cols, yrows, k, after(y_came[k], dsum_other[-1])), "expert", -k)
+        for k in range(1, n_exp)
+    ]
+    dnormed_two = jnp.concatenate(
+        [own.astype(F32) + other.astype(F32) for own, other in zip(dsum, dsum_other)], axis=1
+    )
     scaled = dnormed_two * gain_two
     grad_gain_two = jnp.sum(dnormed_two * unit_two, axis=0)
     dmiddle = grad_full.astype(F32) + scale_two * (
@@ -673,8 +686,8 @@
         - jnp.mean(scaled, axis=-1, keepdims=True)
         - unit_two * jnp.mean(scaled * unit_two, axis=-1, keepdims=True)
     )
-    late = ring_middle(last, arrived_last, dsum_other)
-    datt = after(dmiddle.astype(BF16), late)
+    late = ring_middle(last, arrived_last, dsum_other[-1])
+    datt = after(dmiddle.astype(BF16), late, *y_came)
 
     dside = jnp.concatenate(
         [drouter, jnp.zeros((1, model), F32), grad_gain_two[None, :],
@@ -683,7 +696,11 @@
     dnorm, stats, dpack = attend_back(
         inputs, gain_one, datt, qkv, ctx, pack, dside, expert_count, width, images, seq, n_heads
     )
-    dpack = after(dpack, y_own, down_last)
+    dpack = after(dpack, *y_from, down_last)
+    y_own = combine(slot_cols, yrows, 0, after(y_came[0], dpack)).astype(F32)
+    for value in y_from:
+        y_own = y_own + value.astype(F32)
+    y_own = y_own.astype(BF16)
 
     dpack = dpack.reshape(n_z, CORES, n_exp, shard, columns)
     dsent = swap_core(take(dpack, 1 - core, 1))
@@ -712,8 +729,9 @@
     sums = stats[:, :2].T
     sums_total = sums
     for k in range(1, n_heads):
-        dn_own = dn_own + shift(take(dnorm, (head + k) % n_heads), "heads", k).astype(F32)
-        sums_total = sums_total + shift(sums, "heads", k)
+        came = shift(take(dnorm, (head + k) % n_heads), "heads", k)
+        dn_own = dn_own + after(came, dtotal).astype(F32)
+        sums_total = sums_total + after(shift(sums, "heads", k), dtotal)
     unit_one, scale_one = norm_parts(inputs.astype(F32))
     grad_in = own_half(dmiddle) + scale_one * (
         dn_own * own_half(gain_one)
@@ -725,7 +743,7 @@
     for k in range(1, n_heads):
         there = (head + k) % n_heads
         part_y = lax.dynamic_slice_in_dim(y_own, there * half_width, half_width, 1)
-        y_total = y_total + shift(part_y, "heads", k).astype(F32)
+        y_total = y_total + after(shift(part_y, "heads", k), dtotal).astype(F32)
     block_out = own_half(middle) + y_total
 
     stacked = jnp.stack(ends).reshape(local, 2, CORES, part_rows, hidden_width)

time: 514 us -> 489 us (0.951)
  waiting for transfers between devices: 180 us -> 164 us
  local copies, waits for them, and re-layouts: 53.1 us -> 43.7 us
    ppermute x18, waiting for transfers between devices: 111 us -> 89 us  [shift_z(): return lax.ppermute(value, 'dp', pairs)]
    ppermute x15 -> x17, waiting for transfers between devices: 68.7 us -> 74.1 us  [shift(): lax.ppermute(value, axis, [(i, (i + step) % size) for i in range(size)])]
    ppermute x15 -> x17, starting transfers between devices: 15.6 us -> 18.3 us  [shift(): lax.ppermute(value, axis, [(i, (i + step) % size) for i in range(size)])]
  transfers between devices with their start and end apart: 47 -> 51, of which waited for: 17 -> 21; matrix products, arithmetic and copies ran while one was open for 15% -> 16% of each run, Pallas kernels for 28% -> 30%
where the time goes in v1:
time: 489 us; the launch traced here: 479 us
  waiting for transfers between devices  164 us (34%)
  Pallas kernels  150 us (31%)
  starting transfers between devices  65.8 us (13%)
  other arithmetic  53.7 us (11%)
  local copies, waits for them, and re-layouts  43.7 us (9%)
    ppermute x18, waiting for transfers between devices, shift_z(): return lax.ppermute(value, 'dp', pairs)  89 us
    ppermute x17, waiting for transfers between devices, shift(): lax.ppermute(value, axis, [(i, (i + step) % size) for i in range(size)])  74.1 us
    pallas_call x2, Pallas kernels, run_expert(): pl.pallas_call(functools.partial(expert_kernel, depth, blocks), grid_spec...  56.1 us
    ppermute x18, starting transfers between devices, shift_z(): return lax.ppermute(value, 'dp', pairs)  44.8 us
    pallas_call x2, Pallas kernels, weight_grad(): pl.pallas_call(functools.partial(weight_grad_kernel, depth), grid_spec=pl...  24.1 us
    pallas_call x4, Pallas kernels, combine_back(): pl.pallas_call(functools.partial(combine_back_kernel, local, add is not N...  22.4 us
    pallas_call x1, Pallas kernels, attend_back(): pl.pallas_call(functools.partial(attend_back_kernel, seq, gain_at), grid=...  20.5 us
    ppermute x17, starting transfers between devices, shift(): lax.ppermute(value, axis, [(i, (i + step) % size) for i in range(size)])  18.3 us
  transfers between devices with their start and end apart: 51, of which 21 were waited for; matrix products, arithmetic and copies ran while one was open for 16% of the time, Pallas kernels for 30%

profile of v1, /device:TPU:0, one launch (start us, length us, event | category | flops | bytes accessed | tf_op | source)
XLA Modules:
  0.0 479.4 jit_solution(2757661208395022908)
XLA Ops:
  16.5 5.6 %collective-permute-done = bf16[832,384]{1,0:T(8,128)(2,1)} collective-permute-done((bf16[832,384]{1,0:T(8,128)(2,1)S(1)}, bf16[832,384]{1,0:T(8,128)(2,1)}, u32[]{:S(2)}, u32[]{:S(2)}) %collective-permute-start) | collective-permute-done | bytes 639008 | tf_op jit(solution)/shard_map/ppermute | solution.py:479
  33.2 11.4 %collective-permute-done.8 = bf16[4,48,1664]{2,1,0:T(8,128)(2,1)S(1)} collective-permute-done((bf16[4,48,1664]{2,1,0:T(8,128)(2,1)}, bf16[4,48,1664]{2,1,0:T(8,128)(2,1)S(1)}, u32[]{:S(2)}, u32[]{:S(2)}) %collective-permute-start.8) | collective-permute-done | bytes 639008 | tf_op jit(solution)/shard_map/ppermute | solution.py:479
  46.0 15.5 %collective-permute-done.9.refs_9_.refs_13_ = bf16[2,192,1536]{2,1,0:T(8,128)(2,1)} collective-permute-done((bf16[2,192,1536]{2,1,0:T(8,128)(2,1)}, bf16[2,192,1536]{2,1,0:T(8,128)(2,1)}, u32[]{:S(2)}, u32[]{:S(2)}) %collective-permute-start.9) | collective-permute-done | bytes 1179680 | tf_op jit(solution)/shard_map/ppermute | solution.py:485
  63.0 15.6 %collective-permute-done.11 = bf16[832,384]{1,0:T(8,128)(2,1)} collective-permute-done((bf16[832,384]{1,0:T(8,128)(2,1)S(1)}, bf16[832,384]{1,0:T(8,128)(2,1)}, u32[]{:S(2)}, u32[]{:S(2)}) %collective-permute-start.11) | collective-permute-done | bytes 639008 | tf_op jit(solution)/shard_map/ppermute | solution.py:479
  88.2 10.8 %attend.1 = (bf16[832,768]{1,0:T(8,128)(2,1)}, bf16[832,1152]{1,0:T(8,128)(2,1)}, bf16[832,384]{1,0:T(8,128)(2,1)}) custom-call(bf16[832,768]{1,0:T(8,128)(2,1)} %pad_maximum_fusion.3.x_ref, f32[1,768]{1,0:T(1,128)} %copy.214.gain_ref, bf16[768,1664]{1,0:T(8,128)(2,1)} %bitcast.146, bf16[768,1664]{1,0:T(8,128)(2,1)} %bitcast.147), custom_call_target="tpu_custom_call" | custom-call | flops 38338560 | bytes 79872 | tf_op jit(solution)/shard_map/attend/pallas_call | solution.py:89
  99.0 11.6 %collective-permute-done.12.refs_11_.refs_15_ = bf16[2,192,1536]{2,1,0:T(8,128)(2,1)} collective-permute-done((bf16[2,192,1536]{2,1,0:T(8,128)(2,1)}, bf16[2,192,1536]{2,1,0:T(8,128)(2,1)}, u32[]{:S(2)}, u32[]{:S(2)}) %collective-permute-start.12) | collective-permute-done | bytes 1179680 | tf_op jit(solution)/shard_map/ppermute | solution.py:485
  119.4 15.4 %collective-permute-done.14.refs_10_.refs_14_ = bf16[2,192,1536]{2,1,0:T(8,128)(2,1)} collective-permute-done((bf16[2,192,1536]{2,1,0:T(8,128)(2,1)}, bf16[2,192,1536]{2,1,0:T(8,128)(2,1)}, u32[]{:S(2)}, u32[]{:S(2)}) %collective-permute-start.14) | collective-permute-done | bytes 1179680 | tf_op jit(solution)/shard_map/ppermute | solution.py:485
  149.0 21.8 %collective-permute-done.16.refs_9_.refs_13_ = bf16[2,192,1536]{2,1,0:T(8,128)(2,1)S(1)} collective-permute-done((bf16[2,192,1536]{2,1,0:T(8,128)(2,1)S(1)}, bf16[2,192,1536]{2,1,0:T(8,128)(2,1)S(1)}, u32[]{:S(2)}, u32[]{:S(2)}) %collective-permute-start.16) | collective-permute-done | bytes 1179680 | tf_op jit(solution)/shard_map/ppermute | solution.py:485
  181.4 28.1 %expert.2 = (bf16[2,4,288,768]{3,2,1,0:T(8,128)(2,1)}, bf16[2,4,288,1536]{3,2,1,0:T(8,128)(2,1)}, f32[4,1,832]{2,1,0:T(1,128)}, bf16[4,288,768]{2,1,0:T(8,128)(2...) custom-call(s32[2]{0:T(128)} %pad_add_fusion.1.place_ref, s32[4,1,832]{2,1,0:T(1,128)} %copy.219.slot_ref, ...), custom_call_target="tpu_custom_call" | custom-call | flops 215875584 | bytes 221184 | tf_op jit(solution)/shard_map/expert/pallas_call | solution.py:296
  209.4 11.9 %weight_grad.2 = (bf16[2,192,1536]{2,1,0:T(8,128)(2,1)}, bf16[2,192,1536]{2,1,0:T(8,128)(2,1)}, bf16[2,192,1536]{2,1,0:T(8,128)(2,1)}, bf16[2,192,1536]{2,1,0:T(8,128)(2,1)}) custom-call(s32[2]{0:T(128)} %pad_add_fusion.1.place_ref, bf16[2,4,288,768]{3,2,1,0:T(8,128)(2,1)} %get-tuple-element.83.rows_ref, bf16[2,4,288,1536]{3,2,1,0:T(8,128)(2,1)} %get-tuple-element.84.cols_ref), custom_call_target="tpu_custom_call" | custom-call | flops 84934656 | bytes 239616 | tf_op jit(solution)/shard_map/weight_grad/pallas_call | solution.py:344
  233.0 28.0 %expert.3 = (bf16[2,4,288,768]{3,2,1,0:T(8,128)(2,1)}, bf16[2,4,288,1536]{3,2,1,0:T(8,128)(2,1)}, f32[4,1,832]{2,1,0:T(1,128)}, bf16[4,288,768]{2,1,0:T(8,128)(2...) custom-call(s32[2]{0:T(128)} %pad_add_fusion.2.place_ref, s32[4,1,832]{2,1,0:T(1,128)} %copy.221.slot_ref, ...), custom_call_target="tpu_custom_call" | custom-call | flops 215875584 | bytes 221184 | tf_op jit(solution)/shard_map/expert/pallas_call | solution.py:296
  261.1 12.2 %weight_grad.3 = (bf16[2,192,1536]{2,1,0:T(8,128)(2,1)}, bf16[2,192,1536]{2,1,0:T(8,128)(2,1)}, bf16[2,192,1536]{2,1,0:T(8,128)(2,1)}, bf16[2,192,1536]{2,1,0:T(8,128)(2,1)}) custom-call(s32[2]{0:T(128)} %pad_add_fusion.2.place_ref, bf16[2,4,288,768]{3,2,1,0:T(8,128)(2,1)} %get-tuple-element.90.rows_ref, bf16[2,4,288,1536]{3,2,1,0:T(8,128)(2,1)} %get-tuple-element.91.cols_ref), custom_call_target="tpu_custom_call" | custom-call | flops 84934656 | bytes 239616 | tf_op jit(solution)/shard_map/weight_grad/pallas_call | solution.py:344
  274.8 8.4 %collective-permute-done.23 = bf16[2,192,1536]{2,1,0:T(8,128)(2,1)} collective-permute-done((bf16[2,192,1536]{2,1,0:T(8,128)(2,1)}, bf16[2,192,1536]{2,1,0:T(8,128)(2,1)}, u32[]{:S(2)}, u32[]{:S(2)}) %collective-permute-start.23) | collective-permute-done | bytes 1179680 | tf_op jit(solution)/shard_map/ppermute | solution.py:485
  283.2 5.4 %combine_back.6 = (bf16[832,384]{1,0:T(8,128)(2,1)}, bf16[832,384]{1,0:T(8,128)(2,1)}, f32[8,768]{1,0:T(8,128)}) custom-call(s32[2]{0:T(128)} %pad_add_fusion.1.place_ref, s32[4,832,2]{2,1,0:T(8,128)} %bitcast.137, bf16[4,288,768]{2,1,0:T(8,128)(2,1)} %get-tuple-element.93.refs_0_, bf16[4,288,768]{2,1,0:T(8,128)(2,1)} %get-tuple-element.94.refs_1_, ...), custom_call_target="tpu_custom_call" | custom-call | flops 11501568 | bytes 73728 | tf_op jit(solution)/shard_map/combine_back/pallas_call | solution.py:432
  289.7 5.4 %combine_back.4 = (bf16[832,384]{1,0:T(8,128)(2,1)}, bf16[832,384]{1,0:T(8,128)(2,1)}, f32[8,768]{1,0:T(8,128)}) custom-call(s32[2]{0:T(128)} %pad_add_fusion.1.place_ref, s32[4,832,2]{2,1,0:T(8,128)} %bitcast.138, bf16[4,288,768]{2,1,0:T(8,128)(2,1)} %get-tuple-element.93.refs_0_, bf16[4,288,768]{2,1,0:T(8,128)(2,1)} %get-tuple-element.94.refs_1_, ...), custom_call_target="tpu_custom_call" | custom-call | flops 11501568 | bytes 73728 | tf_op jit(solution)/shard_map/combine_back/pallas_call | solution.py:432
  297.4 5.8 %combine_back.7 = (bf16[832,384]{1,0:T(8,128)(2,1)}, bf16[832,384]{1,0:T(8,128)(2,1)}, f32[8,768]{1,0:T(8,128)}) custom-call(s32[2]{0:T(128)} %pad_add_fusion.1.place_ref, s32[4,832,2]{2,1,0:T(8,128)} %bitcast.139, bf16[4,288,768]{2,1,0:T(8,128)(2,1)} %get-tuple-element.93.refs_0_, bf16[4,288,768]{2,1,0:T(8,128)(2,1)} %get-tuple-element.94.refs_1_, ...), custom_call_target="tpu_custom_call" | custom-call | flops 11501568 | bytes 73728 | tf_op jit(solution)/shard_map/combine_back/pallas_call | solution.py:432
  306.6 5.8 %combine_back.5 = (bf16[832,384]{1,0:T(8,128)(2,1)}, bf16[832,384]{1,0:T(8,128)(2,1)}, f32[8,768]{1,0:T(8,128)}) custom-call(s32[2]{0:T(128)} %pad_add_fusion.1.place_ref, s32[4,832,2]{2,1,0:T(8,128)} %bitcast.140, bf16[4,288,768]{2,1,0:T(8,128)(2,1)} %get-tuple-element.93.refs_0_, bf16[4,288,768]{2,1,0:T(8,128)(2,1)} %get-tuple-element.94.refs_1_, ...), custom_call_target="tpu_custom_call" | custom-call | flops 11501568 | bytes 73728 | tf_op jit(solution)/shard_map/combine_back/pallas_call | solution.py:432
  312.4 8.2 %collective-permute-done.30 = bf16[832,384]{1,0:T(8,128)(2,1)S(1)} collective-permute-done((bf16[832,384]{1,0:T(8,128)(2,1)}, bf16[832,384]{1,0:T(8,128)(2,1)S(1)}, u32[]{:S(2)}, u32[]{:S(2)}) %collective-permute-start.30) | collective-permute-done | bytes 639008 | tf_op jit(solution)/shard_map/ppermute | solution.py:479
  327.0 6.5 %collective-permute-done.33 = bf16[832,384]{1,0:T(8,128)(2,1)} collective-permute-done((bf16[832,384]{1,0:T(8,128)(2,1)}, bf16[832,384]{1,0:T(8,128)(2,1)}, u32[]{:S(2)}, u32[]{:S(2)}) %collective-permute-start.33) | collective-permute-done | bytes 639008 | tf_op jit(solution)/shard_map/ppermute | solution.py:479
  364.9 20.5 %attend_back.1 = (bf16[2,832,384]{2,1,0:T(8,128)(2,1)}, f32[832,128]{1,0:T(8,128)}, bf16[768,1664]{1,0:T(8,128)(2,1)}) custom-call(bf16[832,768]{1,0:T(8,128)(2,1)} %pad_maximum_fusion.3.x_ref, f32[1,768]{1,0:T(1,128)} %copy.214.gain_ref, bf16[832,768]{1,0:T(8,128)(2,1)} %get-tuple-element.113.datt_ref, bf16[832,1152]{1,0:T(8,128)(2,1)} %get-tuple-element.114.qkv_ref, ...), custom_call_target="tpu_custom_call" | custom-call | flops 107347968 | bytes 119808 | tf_op jit(solution)/shard_map/attend_back/pallas_call | solution.py:180
  407.0 8.2 %collective-permute-done.42 = bf16[4,48,1664]{2,1,0:T(8,128)(2,1)} collective-permute-done((bf16[4,48,1664]{2,1,0:T(8,128)(2,1)}, bf16[4,48,1664]{2,1,0:T(8,128)(2,1)}, u32[]{:S(2)}, u32[]{:S(2)}) %collective-permute-start.42) | collective-permute-done | bytes 639008 | tf_op jit(solution)/shard_map/ppermute | solution.py:479
  416.6 22.5 %collective-permute-start.45 = (bf16[48,1664]{1,0:T(8,128)(2,1)S(1)}, bf16[48,1664]{1,0:T(8,128)(2,1)S(1)}, u32[]{:S(2)}, u32[]{:S(2)}) collective-permute-start(bf16[48,1664]{1,0:T(8,128)(2,1)S(1)} %get-tuple-element.217), channel_id=1, source_target_pairs={{0,24},{4,28},{8,0},{12,4},{16,8},{20,12},{24,16},{28,20},{1,25},{... | collective-permute-start | bytes 479240 | tf_op jit(solution)/shard_map/ppermute | solution.py:485
  446.9 8.9 %collective-permute-done.44 = bf16[48,1664]{1,0:T(8,128)(2,1)S(1)} collective-permute-done((bf16[48,1664]{1,0:T(8,128)(2,1)S(1)}, bf16[48,1664]{1,0:T(8,128)(2,1)S(1)}, u32[]{:S(2)}, u32[]{:S(2)}) %collective-permute-start.44) | collective-permute-done | bytes 159776 | tf_op jit(solution)/shard_map/ppermute | solution.py:485
  457.2 4.8 %collective-permute-done.40 = bf16[832,384]{1,0:T(8,128)(2,1)S(1)} collective-permute-done((bf16[832,384]{1,0:T(8,128)(2,1)S(1)}, bf16[832,384]{1,0:T(8,128)(2,1)S(1)}, u32[]{:S(2)}, u32[]{:S(2)}) %collective-permute-start.40) | collective-permute-done | bytes 639008 | tf_op jit(solution)/shard_map/ppermute | solution.py:479
  (303 shorter events, 179.4 us)
Async XLA Ops:
  31.7 29.8 %collective-permute-start.9 = (bf16[2,192,1536]{2,1,0:T(8,128)(2,1)}, bf16[2,192,1536]{2,1,0:T(8,128)(2,1)}, u32[]{:S(2)}, u32[]{:S(2)}) collective-permute-start(bf16[2,192,1536]{2,1,0:T(8,128)(2,1)} %get-tuple-element.203.refs_8_.refs_12_), channel_id=1, source_target_pairs={{0,8},{4,12},{8,16},{12,20},{16,24},{20,28},{24,0},{28,4},{1,9},{5... | collective-permute-start | bytes 3538952 | tf_op jit(solution)/shard_map/ppermute | solution.py:485
  81.6 29.0 %collective-permute-start.12 = (bf16[2,192,1536]{2,1,0:T(8,128)(2,1)}, bf16[2,192,1536]{2,1,0:T(8,128)(2,1)}, u32[]{:S(2)}, u32[]{:S(2)}) collective-permute-start(bf16[2,192,1536]{2,1,0:T(8,128)(2,1)} %get-tuple-element.203.refs_8_.refs_12_), channel_id=1, source_target_pairs={{0,24},{4,28},{8,0},{12,4},{16,8},{20,12},{24,16},{28,20},{1,25},{... | collective-permute-start | bytes 3538952 | tf_op jit(solution)/shard_map/ppermute | solution.py:485
  83.3 51.5 %collective-permute-start.14 = (bf16[2,192,1536]{2,1,0:T(8,128)(2,1)}, bf16[2,192,1536]{2,1,0:T(8,128)(2,1)}, u32[]{:S(2)}, u32[]{:S(2)}) collective-permute-start(bf16[2,192,1536]{2,1,0:T(8,128)(2,1)} %collective-permute-done.9.refs_9_.refs_13_), channel_id=1, source_target_pairs={{0,8},{4,12},{8,16},{12,20},{16,24},{20,28},{24,0},{28,4},{1,9},{5... | collective-permute-start | bytes 3538952 | tf_op jit(solution)/shard_map/ppermute | solution.py:485
  110.6 28.1 %collective-permute-start.13 = (bf16[832,768]{1,0:T(8,128)(2,1)}, bf16[832,768]{1,0:T(8,128)(2,1)}, u32[]{:S(2)}, u32[]{:S(2)}) collective-permute-start(bf16[832,768]{1,0:T(8,128)(2,1)} %get-tuple-element.77), channel_id=1, source_target_pairs={{0,2},{2,0},{1,3},{3,1},{4,6},{6,4},{5,7},{7,5},{8,10},{10,8},{9,1... | collective-permute-start | bytes 3833864 | tf_op jit(solution)/shard_map/ppermute | solution.py:479
  118.4 30.1 %collective-permute-start.19 = (bf16[832,768]{1,0:T(8,128)(2,1)}, bf16[832,768]{1,0:T(8,128)(2,1)}, u32[]{:S(2)}, u32[]{:S(2)}) collective-permute-start(bf16[832,768]{1,0:T(8,128)(2,1)} %pad_maximum_fusion.5.refs_4_), channel_id=1, source_target_pairs={{0,1},{1,0},{2,3},{3,2},{4,5},{5,4},{6,7},{7,6},{8,9},{9,8},{10,11... | collective-permute-start | bytes 3833864 | tf_op jit(solution)/shard_map/ppermute | solution.py:479
  144.0 29.5 %collective-permute-start.15 = (bf16[832,768]{1,0:T(8,128)(2,1)}, bf16[832,768]{1,0:T(8,128)(2,1)}, u32[]{:S(2)}, u32[]{:S(2)}) collective-permute-start(bf16[832,768]{1,0:T(8,128)(2,1)} %multiply_convert_fusion.refs_0_.refs_6_), channel_id=1, source_target_pairs={{0,1},{1,0},{2,3},{3,2},{4,5},{5,4},{6,7},{7,6},{8,9},{9,8},{10,11... | collective-permute-start | bytes 3833864 | tf_op jit(solution)/shard_map/ppermute | solution.py:479
  144.6 26.2 %collective-permute-start.16 = (bf16[2,192,1536]{2,1,0:T(8,128)(2,1)S(1)}, bf16[2,192,1536]{2,1,0:T(8,128)(2,1)S(1)}, u32[]{:S(2)}, u32[]{:S(2)}) collective-permute-start(bf16[2,192,1536]{2,1,0:T(8,128)(2,1)S(1)} %copy-done.5), channel_id=1, source_target_pairs={{0,8},{4,12},{8,16},{12,20},{16,24},{20,28},{24,0},{28,4},{1,9},{5... | collective-permute-start | bytes 3538952 | tf_op jit(solution)/shard_map/ppermute | solution.py:485
  144.6 36.5 %collective-permute-start.20 = (bf16[832,768]{1,0:T(8,128)(2,1)}, bf16[832,768]{1,0:T(8,128)(2,1)}, u32[]{:S(2)}, u32[]{:S(2)}) collective-permute-start(bf16[832,768]{1,0:T(8,128)(2,1)} %pad_maximum_fusion.5.refs_4_), channel_id=1, source_target_pairs={{0,4},{4,0},{8,12},{12,8},{16,20},{20,16},{24,28},{28,24},{1,5},{5... | collective-permute-start | bytes 3833864 | tf_op jit(solution)/shard_map/ppermute | solution.py:488
  148.5 32.8 %collective-permute-start.21 = (bf16[832,768]{1,0:T(8,128)(2,1)}, bf16[832,768]{1,0:T(8,128)(2,1)}, u32[]{:S(2)}, u32[]{:S(2)}) collective-permute-start(bf16[832,768]{1,0:T(8,128)(2,1)} %collective-permute-done.19.refs_5_), channel_id=1, source_target_pairs={{0,4},{4,0},{8,12},{12,8},{16,20},{20,16},{24,28},{28,24},{1,5},{5... | collective-permute-start | bytes 3833864 | tf_op jit(solution)/shard_map/ppermute | solution.py:488
  148.5 32.8 %collective-permute-start.17 = (bf16[832,768]{1,0:T(8,128)(2,1)}, bf16[832,768]{1,0:T(8,128)(2,1)}, u32[]{:S(2)}, u32[]{:S(2)}) collective-permute-start(bf16[832,768]{1,0:T(8,128)(2,1)} %multiply_convert_fusion.refs_0_.refs_6_), channel_id=1, source_target_pairs={{0,4},{4,0},{8,12},{12,8},{16,20},{20,16},{24,28},{28,24},{1,5},{5... | collective-permute-start | bytes 3833864 | tf_op jit(solution)/shard_map/ppermute | solution.py:488
  176.8 52.0 %collective-permute-start.25 = (bf16[2,192,1536]{2,1,0:T(8,128)(2,1)}, bf16[2,192,1536]{2,1,0:T(8,128)(2,1)}, u32[]{:S(2)}, u32[]{:S(2)}) collective-permute-start(bf16[2,192,1536]{2,1,0:T(8,128)(2,1)} %get-tuple-element.89.refs_8_.refs_12_), channel_id=1, source_target_pairs={{0,24},{4,28},{8,0},{12,4},{16,8},{20,12},{24,16},{28,20},{1,25},{... | collective-permute-start | bytes 3538952 | tf_op jit(solution)/shard_map/ppermute | solution.py:485
  181.1 51.9 %collective-permute-start.24 = (bf16[2,192,1536]{2,1,0:T(8,128)(2,1)}, bf16[2,192,1536]{2,1,0:T(8,128)(2,1)}, u32[]{:S(2)}, u32[]{:S(2)}) collective-permute-start(bf16[2,192,1536]{2,1,0:T(8,128)(2,1)} %copy-done.14), channel_id=1, source_target_pairs={{0,8},{4,12},{8,16},{12,20},{16,24},{20,28},{24,0},{28,4},{1,9},{5... | collective-permute-start | bytes 3538952 | tf_op jit(solution)/shard_map/ppermute | solution.py:485
  221.3 51.9 %collective-permute-start.22 = (bf16[2,192,1536]{2,1,0:T(8,128)(2,1)}, bf16[2,192,1536]{2,1,0:T(8,128)(2,1)}, u32[]{:S(2)}, u32[]{:S(2)}) collective-permute-start(bf16[2,192,1536]{2,1,0:T(8,128)(2,1)} %get-tuple-element.85), channel_id=1, source_target_pairs={{0,8},{4,12},{8,16},{12,20},{16,24},{20,28},{24,0},{28,4},{1,9},{5... | collective-permute-start | bytes 3538952 | tf_op jit(solution)/shard_map/ppermute | solution.py:485
  221.3 61.9 %collective-permute-start.23 = (bf16[2,192,1536]{2,1,0:T(8,128)(2,1)}, bf16[2,192,1536]{2,1,0:T(8,128)(2,1)}, u32[]{:S(2)}, u32[]{:S(2)}) collective-permute-start(bf16[2,192,1536]{2,1,0:T(8,128)(2,1)} %get-tuple-element.87), channel_id=1, source_target_pairs={{0,24},{4,28},{8,0},{12,4},{16,8},{20,12},{24,16},{28,20},{1,25},{... | collective-permute-start | bytes 3538952 | tf_op jit(solution)/shard_map/ppermute | solution.py:485
  289.1 34.7 %collective-permute-start.32 = (bf16[2,192,1536]{2,1,0:T(8,128)(2,1)S(1)}, bf16[2,192,1536]{2,1,0:T(8,128)(2,1)S(1)}, u32[]{:S(2)}, u32[]{:S(2)}) collective-permute-start(bf16[2,192,1536]{2,1,0:T(8,128)(2,1)S(1)} %add_convert_fusion.2), channel_id=1, source_target_pairs={{0,8},{4,12},{8,16},{12,20},{16,24},{20,28},{24,0},{28,4},{1,9},{5... | collective-permute-start | bytes 3538952 | tf_op jit(solution)/shard_map/ppermute | solution.py:485
  303.6 45.1 %collective-permute-start.36 = (bf16[2,192,1536]{2,1,0:T(8,128)(2,1)}, bf16[2,192,1536]{2,1,0:T(8,128)(2,1)}, u32[]{:S(2)}, u32[]{:S(2)}) collective-permute-start(bf16[2,192,1536]{2,1,0:T(8,128)(2,1)} %get-tuple-element.109), channel_id=1, source_target_pairs={{0,8},{4,12},{8,16},{12,20},{16,24},{20,28},{24,0},{28,4},{1,9},{5... | collective-permute-start | bytes 3538952 | tf_op jit(solution)/shard_map/ppermute | solution.py:485
  304.3 29.2 %collective-permute-start.33 = (bf16[832,384]{1,0:T(8,128)(2,1)}, bf16[832,384]{1,0:T(8,128)(2,1)}, u32[]{:S(2)}, u32[]{:S(2)}) collective-permute-start(bf16[832,384]{1,0:T(8,128)(2,1)} %get-tuple-element.108), channel_id=1, source_target_pairs={{0,1},{1,0},{2,3},{3,2},{4,5},{5,4},{6,7},{7,6},{8,9},{9,8},{10,11... | collective-permute-start | bytes 1916936 | tf_op jit(solution)/shard_map/ppermute | solution.py:479
  322.9 26.4 %collective-permute-start.35 = (bf16[832,384]{1,0:T(8,128)(2,1)S(1)}, bf16[832,384]{1,0:T(8,128)(2,1)}, u32[]{:S(2)}, u32[]{:S(2)}) collective-permute-start(bf16[832,384]{1,0:T(8,128)(2,1)S(1)} %add_convert_fusion.5), channel_id=1, source_target_pairs={{0,2},{2,0},{1,3},{3,1},{4,6},{6,4},{5,7},{7,5},{8,10},{10,8},{9,1... | collective-permute-start | bytes 1916936 | tf_op jit(solution)/shard_map/ppermute | solution.py:479
  336.6 48.8 %collective-permute-start.39 = (bf16[2,192,1536]{2,1,0:T(8,128)(2,1)}, bf16[2,192,1536]{2,1,0:T(8,128)(2,1)}, u32[]{:S(2)}, u32[]{:S(2)}) collective-permute-start(bf16[2,192,1536]{2,1,0:T(8,128)(2,1)} %get-tuple-element.122), channel_id=1, source_target_pairs={{0,24},{4,28},{8,0},{12,4},{16,8},{20,12},{24,16},{28,20},{1,25},{... | collective-permute-start | bytes 3538952 | tf_op jit(solution)/shard_map/ppermute | solution.py:485
  359.3 29.4 %collective-permute-start.38 = (bf16[832,768]{1,0:T(8,128)(2,1)}, bf16[832,768]{1,0:T(8,128)(2,1)S(1)}, u32[]{:S(2)}, u32[]{:S(2)}) collective-permute-start(bf16[832,768]{1,0:T(8,128)(2,1)} %combine.6), channel_id=1, source_target_pairs={{0,1},{1,0},{2,3},{3,2},{4,5},{5,4},{6,7},{7,6},{8,9},{9,8},{10,11... | collective-permute-start | bytes 3833864 | tf_op jit(solution)/shard_map/ppermute | solution.py:479
  392.5 49.9 %collective-permute-start.49 = (bf16[2,192,1536]{2,1,0:T(8,128)(2,1)}, bf16[2,192,1536]{2,1,0:T(8,128)(2,1)S(1)}, u32[]{:S(2)}, u32[]{:S(2)}) collective-permute-start(bf16[2,192,1536]{2,1,0:T(8,128)(2,1)} %add_convert_fusion.1), channel_id=1, source_target_pairs={{0,8},{4,12},{8,16},{12,20},{16,24},{20,28},{24,0},{28,4},{1,9},{5... | collective-permute-start | bytes 3538952 | tf_op jit(solution)/shard_map/ppermute | solution.py:485
  393.9 63.3 %collective-permute-start.46 = (bf16[832,384]{1,0:T(8,128)(2,1)S(1)}, bf16[832,384]{1,0:T(8,128)(2,1)S(1)}, u32[]{:S(2)}, u32[]{:S(2)}) collective-permute-start(bf16[832,384]{1,0:T(8,128)(2,1)S(1)} %dynamic-slice_bitcast_fusion.1), channel_id=1, source_target_pairs={{0,2},{2,0},{1,3},{3,1},{4,6},{6,4},{5,7},{7,5},{8,10},{10,8},{9,1... | collective-permute-start | bytes 1916936 | tf_op jit(solution)/shard_map/ppermute | solution.py:479
  399.8 56.1 %collective-permute-start.47 = (f32[2,832]{0,1:T(8,128)}, f32[2,832]{0,1:T(8,128)}, u32[]{:S(2)}, u32[]{:S(2)}) collective-permute-start(f32[2,832]{0,1:T(8,128)} %slice_bitcast_fusion.2), channel_id=1, source_target_pairs={{0,2},{2,0},{1,3},{3,1},{4,6},{6,4},{5,7},{7,5},{8,10},{10,8},{9,1... | collective-permute-start | bytes 19976 | tf_op jit(solution)/shard_map/ppermute | solution.py:479
  416.6 29.5 %collective-permute-start.45 = (bf16[48,1664]{1,0:T(8,128)(2,1)S(1)}, bf16[48,1664]{1,0:T(8,128)(2,1)S(1)}, u32[]{:S(2)}, u32[]{:S(2)}) collective-permute-start(bf16[48,1664]{1,0:T(8,128)(2,1)S(1)} %get-tuple-element.217), channel_id=1, source_target_pairs={{0,24},{4,28},{8,0},{12,4},{16,8},{20,12},{24,16},{28,20},{1,25},{... | collective-permute-start | bytes 479240 | tf_op jit(solution)/shard_map/ppermute | solution.py:485
  (77 other events, 612.4 us)
